TPU v7x, 256 devices: a whole 4x4x8 slice. The times are simulated.
256 devices in a mesh: dp: 8 (over z), blk: 8 (over y_hi, x), mp: 4 (over y_lo, core).
Axes of the slice: x: 4, y: 4 (y_hi: 2, y_lo: 2; y = y_hi * 2 + y_lo), z: 8, core: 2. Of those that a mesh axis runs over, the one named last changes fastest.
Arguments:
- encoder_query: bfloat16 [8, 2048, 2048], P('dp', 'blk', 'mp'), may hold values from -0.4296875 to 0.4296875
- encoder_keys: bfloat16 [8, 2048, 2048], P('dp', 'blk', 'mp'), may hold values from -0.4296875 to 0.4296875
- encoder_values: bfloat16 [8, 2048, 2048], P('dp', 'blk', 'mp'), may hold values from -1.5 to 1.5
- encoder_output: bfloat16 [8, 2048, 2048], P('dp', 'blk', 'mp'), may hold values from -1.5 to 1.5
- encoder_cotangent: bfloat16 [8, 2048, 2048], P('dp', 'blk', 'mp'), may hold values from -96 to 96
- encoder_totals: float32 [8, 8, 2048], P('dp', 'mp', 'blk'), may hold values from 1024 to 4096
- cross_keys: bfloat16 [8, 2048, 2048], P('dp', 'blk', 'mp'), may hold values from -0.4296875 to 0.4296875
- cross_values: bfloat16 [8, 2048, 2048], P('dp', 'blk', 'mp'), may hold values from -1.5 to 1.5
- decoder_query: bfloat16 [8, 256, 2048], P('dp', None, 'mp'), may hold values from -0.4296875 to 0.4296875
- decoder_output: bfloat16 [8, 256, 2048], P('dp', None, 'mp'), may hold values from -1.5 to 1.5
- decoder_cotangent: bfloat16 [8, 256, 2048], P('dp', None, 'mp'), may hold values from -192 to 192
- decoder_totals: float32 [8, 8, 256], P('dp', 'mp'), may hold values from 1024 to 4096
- encoder_states: bfloat16 [8, 2048, 4096], P('dp', 'blk', 'mp'), may hold values from -0.046875 to 0.046875
Outputs:
- encoder_query_grad: bfloat16 [8, 2048, 2048], P('dp', 'blk', 'mp')
- encoder_key_grad: bfloat16 [8, 2048, 2048], P('dp', 'blk', 'mp')
- encoder_value_grad: bfloat16 [8, 2048, 2048], P('dp', 'blk', 'mp')
- cross_key_grad: bfloat16 [8, 2048, 2048], P('dp', 'blk', 'mp')
- cross_value_grad: bfloat16 [8, 2048, 2048], P('dp', 'blk', 'mp')
- decoder_query_grad: bfloat16 [8, 256, 2048], P('dp', None, 'mp')
- value_weight_grad: float32 [4096, 2048], P(('dp', 'blk'), 'mp')
All inputs are finite; a program needn't handle non-finite values.
Results may differ from a plain program's by a relative error of at most 0.005.
Values may be sent and summed in bfloat16 or wider, within the bound.
A program may use at most 128 MiB of HBM per device.

v0:
```python
import jax
import jax.numpy as jnp
from jax import lax
from jax.sharding import PartitionSpec as P

HD = 256


def passed_along(value, axis, steps):
    count = lax.axis_size(axis)
    pairs = [(source, (source + steps) % count) for source in range(count)]
    return lax.ppermute(value, axis, pairs)


def by_heads(array):
    return array.reshape(array.shape[0], array.shape[1] // HD, HD)


def row_statistic(grad_out, outputs):
    return jnp.sum(grad_out.astype(jnp.float32) * outputs.astype(jnp.float32), axis=-1).T


def score_tile(queries, key_rows, values, grad_out, totals, row_delta):
    scores = jnp.einsum("qhd,khd->hqk", queries, key_rows, preferred_element_type=jnp.float32)
    softmax = jnp.exp(scores) / totals[:, :, None]
    weights = softmax.astype(jnp.bfloat16)
    dprobs = jnp.einsum("qhd,khd->hqk", grad_out, values, preferred_element_type=jnp.float32)
    dscores = (softmax * (dprobs - row_delta[:, :, None])).astype(jnp.bfloat16)
    return (weights, dscores)


def query_side(dscores, key_rows):
    return jnp.einsum("hqk,khd->qhd", dscores, key_rows, preferred_element_type=jnp.float32)


def key_side(dscores, queries):
    return jnp.einsum("hqk,qhd->khd", dscores, queries, preferred_element_type=jnp.float32)


def flatten_out(array):
    return array.reshape(1, array.shape[0], array.shape[1] * array.shape[2]).astype(jnp.bfloat16)


def body(
    encoder_query,
    encoder_keys,
    encoder_values,
    encoder_output,
    encoder_cotangent,
    encoder_totals,
    cross_keys,
    cross_values,
    decoder_query,
    decoder_output,
    decoder_cotangent,
    decoder_totals,
    encoder_states,
):
    queries = by_heads(encoder_query[0])
    key_rows = by_heads(encoder_keys[0])
    values = by_heads(encoder_values[0])
    grad_out = by_heads(encoder_cotangent[0])
    totals = encoder_totals[0]
    row_delta = row_statistic(grad_out, by_heads(encoder_output[0]))
    cycle_size = lax.axis_size("blk")
    query_acc = jnp.zeros(queries.shape, jnp.float32)
    key_acc = jnp.zeros(queries.shape, jnp.float32)
    value_acc = jnp.zeros(queries.shape, jnp.float32)
    moving_keys, moving_values = (key_rows, values)
    for section in range(cycle_size):
        weights, dscores = score_tile(
            queries, moving_keys, moving_values, grad_out, totals, row_delta
        )
        query_acc = query_acc + query_side(dscores, moving_keys)
        key_acc = key_acc + key_side(dscores, queries)
        value_acc = value_acc + key_side(weights, grad_out)
        if section + 1 < cycle_size:
            moving_keys, moving_values = passed_along((moving_keys, moving_values), "blk", 1)
        key_acc, value_acc = passed_along((key_acc, value_acc), "blk", 1)
    summary_query = by_heads(decoder_query[0])
    summary_grad_out = by_heads(decoder_cotangent[0])
    summary_delta = row_statistic(summary_grad_out, by_heads(decoder_output[0]))
    cross_rows = by_heads(cross_keys[0])
    cross_vals = by_heads(cross_values[0])
    cross_weights, cross_dscores = score_tile(
        summary_query, cross_rows, cross_vals, summary_grad_out, decoder_totals[0], summary_delta
    )
    summary_part = query_side(cross_dscores, cross_rows)
    summary_total = lax.psum(summary_part, "blk")
    cross_kgrad = flatten_out(key_side(cross_dscores, summary_query))
    cross_vgrad = flatten_out(key_side(cross_weights, summary_grad_out))
    states_all = lax.all_gather(encoder_states[0], "mp", axis=1, tiled=True)
    value_flat = cross_vgrad[0]
    weight_grad = lax.psum_scatter(
        lax.dot_general(
            states_all, value_flat, (((0,), (0,)), ((), ())), preferred_element_type=jnp.float32
        ),
        ("dp", "blk"),
        scatter_dimension=0,
        tiled=True,
    )
    return (
        flatten_out(query_acc),
        flatten_out(key_acc),
        flatten_out(value_acc),
        cross_kgrad,
        cross_vgrad,
        flatten_out(summary_total),
        weight_grad,
    )


def solution(mesh):
    in_specs = (
        P("dp", "blk", "mp"),
        P("dp", "blk", "mp"),
        P("dp", "blk", "mp"),
        P("dp", "blk", "mp"),
        P("dp", "blk", "mp"),
        P("dp", "mp", "blk"),
        P("dp", "blk", "mp"),
        P("dp", "blk", "mp"),
        P("dp", None, "mp"),
        P("dp", None, "mp"),
        P("dp", None, "mp"),
        P("dp", "mp", None),
        P("dp", "blk", "mp"),
    )
    out_specs = (
        P("dp", "blk", "mp"),
        P("dp", "blk", "mp"),
        P("dp", "blk", "mp"),
        P("dp", "blk", "mp"),
        P("dp", "blk", "mp"),
        P("dp", None, "mp"),
        P(("dp", "blk"), "mp"),
    )
    return jax.shard_map(body, mesh=mesh, in_specs=in_specs, out_specs=out_specs, check_vma=False)
```

profile of v0, /device:TPU:8, one launch (start us, length us, event | category | flops | bytes accessed | tf_op | source)
XLA Modules:
  0.0 448.2 jit_solution(9057717714585304565)
XLA Ops:
  7.2 0.7 all-gather.3.cloned.1.call-update
  8.0 1.0 reshape_squeeze.31
  9.0 1.1 reshape_squeeze.32
  10.5 0.3 fusion.11
  11.0 31.7 %all-gather.3.cloned.1.call-done = bf16[1,256,4096]{2,1,0:T(8,128)(2,1)} async-done(((bf16[1,256,1024]{2,1,0:T(8,128)(2,1)}), bf16[1,256,4096]{2,1,0:T(8,128)(2,1)}) %all-gather.3.cloned.1.call-update) | async-done | bytes 2097168 | tf_op jit(solution)/shard_map/all_gather | solution.py:92
  42.7 6.1 %convolution_bitcast_fusion = f32[4096,512]{0,1:T(8,128)} fusion(bf16[256,512]{0,1:T(8,128)(2,1)S(1)} %bitcast.117, bf16[1,256,4096]{2,1,0:T(8,128)(2,1)} %all-gather.3.cloned.1.call-done), kind=kOutput, calls=%fused_computation | convolution fusion | flops 1073741824 | bytes 10747904 | tf_op jit(solution)/shard_map/dot_general | solution.py:95
  48.8 9.1 %copy.270 = f32[4096,512]{1,0:T(8,128)} copy(f32[4096,512]{0,1:T(8,128)} %convolution_bitcast_fusion) | data formatting | bytes 16777216
  57.9 0.9 copy-done.3
  59.0 0.8 copy.174
  59.8 2.1 collective-permute-start.1
  62.0 0.8 copy.172
  62.9 1.5 collective-permute-start
  64.5 0.3 reshape.108
  64.8 0.4 multiply_reduce_fusion.1
  65.8 1.1 convolution_bitcast_fusion.17
  67.0 1.2 collective-permute-start.14
  68.1 1.1 convolution_bitcast_fusion.9
  69.2 2.4 collective-permute-start.22
  71.7 1.3 reshape.109
  72.9 0.4 multiply_reduce_fusion
  73.4 0.3 fusion.29
  73.7 1.2 convolution_bitcast_fusion.1
  74.9 76.4 %all-reduce.1 = bf16[256,2,256]{2,0,1:T(8,128)(2,1)S(1)} all-reduce(f32[256,2,256]{2,0,1:T(8,128)S(1)} %convolution_bitcast_fusion.1), channel_id=1, replica_groups=mesh['dp'=8,'blk'=8,'mp'=4] {'blk'}, use_global_device_ids=true, to_apply=%region_2.0 | all-reduce | flops 131072 | bytes 786432 | tf_op jit(solution)/shard_map/psum | solution.py:89
  151.5 0.8 copy.242
  152.5 0.8 copy.243
  153.3 0.8 copy.241
  154.5 2.6 collective-permute-start.2
  157.1 1.3 fusion.2
  158.4 1.2 fusion.22
  159.6 1.2 convolution_add_fusion.6
  160.8 8.4 %collective-permute-done.2 = bf16[256,2,256]{2,0,1:T(8,128)(2,1)S(1)} collective-permute-done((bf16[256,2,256]{2,0,1:T(8,128)(2,1)}, bf16[256,2,256]{2,0,1:T(8,128)(2,1)S(1)}, u32[]{:S(2)}, u32[]{:S(2)}) %collective-permute-start.2) | collective-permute-done | bytes 262176 | tf_op jit(solution)/shard_map/ppermute | solution.py:12
  169.8 1.3 fusion.9
  171.6 5.4 %collective-permute-start.4 = (bf16[256,2,256]{2,0,1:T(8,128)(2,1)S(1)}, bf16[256,2,256]{2,0,1:T(8,128)(2,1)S(1)}, u32[]{:S(2)}, u32[]{:S(2)}) collective-permute-start(bf16[256,2,256]{2,0,1:T(8,128)(2,1)S(1)} %collective-permute-done.2), channel_id=1, source_target_pairs={{0,4},{4,8},{8,12},{12,16},{16,20},{20,24},{24,28},{28,0},{1,5},{5... | collective-permute-start | bytes 786440 | tf_op jit(solution)/shard_map/ppermute | solution.py:12
  177.2 0.3 convolution_add_fusion.5
  177.5 1.3 fusion.10
  178.9 6.1 %collective-permute-start.23 = (f32[256,2,256]{2,0,1:T(8,128)S(1)}, f32[256,2,256]{2,0,1:T(8,128)S(1)}, u32[]{:S(2)}, u32[]{:S(2)}) collective-permute-start(f32[256,2,256]{2,0,1:T(8,128)S(1)} %fusion.10), channel_id=1, source_target_pairs={{0,4},{4,8},{8,12},{12,16},{16,20},{20,24},{24,28},{28,0},{1,5},{5... | collective-permute-start | bytes 1572872 | tf_op jit(solution)/shard_map/ppermute | solution.py:12
  184.9 24.2 %collective-permute-done.4 = bf16[256,2,256]{2,0,1:T(8,128)(2,1)S(1)} collective-permute-done((bf16[256,2,256]{2,0,1:T(8,128)(2,1)S(1)}, bf16[256,2,256]{2,0,1:T(8,128)(2,1)S(1)}, u32[]{:S(2)}, u32[]{:S(2)}) %collective-permute-start.4) | collective-permute-done | bytes 262176 | tf_op jit(solution)/shard_map/ppermute | solution.py:12
  210.4 0.3 convolution_add_fusion.4
  210.8 5.4 %collective-permute-start.16 = (f32[256,2,256]{2,0,1:T(8,128)S(1)}, f32[256,2,256]{2,0,1:T(8,128)S(1)}, u32[]{:S(2)}, u32[]{:S(2)}) collective-permute-start(f32[256,2,256]{2,0,1:T(8,128)S(1)} %add.82), channel_id=1, source_target_pairs={{0,4},{4,8},{8,12},{12,16},{16,20},{20,24},{24,28},{28,0},{1,5},{5... | collective-permute-start | bytes 1572872 | tf_op jit(solution)/shard_map/ppermute | solution.py:12
  216.1 8.9 %collective-permute-done.23 = f32[256,2,256]{2,0,1:T(8,128)S(1)} collective-permute-done((f32[256,2,256]{2,0,1:T(8,128)S(1)}, f32[256,2,256]{2,0,1:T(8,128)S(1)}, u32[]{:S(2)}, u32[]{:S(2)}) %collective-permute-start.23) | collective-permute-done | bytes 524320 | tf_op jit(solution)/shard_map/ppermute | solution.py:12
  225.2 14.1 %collective-permute-done.6 = bf16[256,2,256]{2,0,1:T(8,128)(2,1)S(1)} collective-permute-done((bf16[256,2,256]{2,0,1:T(8,128)(2,1)S(1)}, bf16[256,2,256]{2,0,1:T(8,128)(2,1)S(1)}, u32[]{:S(2)}, u32[]{:S(2)}) %collective-permute-start.6) | collective-permute-done | bytes 262176 | tf_op jit(solution)/shard_map/ppermute | solution.py:12
  240.9 36.9 %collective-permute-done.9 = bf16[256,2,256]{2,0,1:T(8,128)(2,1)S(1)} collective-permute-done((bf16[256,2,256]{2,0,1:T(8,128)(2,1)S(1)}, bf16[256,2,256]{2,0,1:T(8,128)(2,1)S(1)}, u32[]{:S(2)}, u32[]{:S(2)}) %collective-permute-start.9) | collective-permute-done | bytes 262176 | tf_op jit(solution)/shard_map/ppermute | solution.py:12
  277.9 7.5 %collective-permute-done.8 = bf16[256,2,256]{2,0,1:T(8,128)(2,1)S(1)} collective-permute-done((bf16[256,2,256]{2,0,1:T(8,128)(2,1)S(1)}, bf16[256,2,256]{2,0,1:T(8,128)(2,1)S(1)}, u32[]{:S(2)}, u32[]{:S(2)}) %collective-permute-start.8) | collective-permute-done | bytes 262176 | tf_op jit(solution)/shard_map/ppermute | solution.py:12
  286.0 4.5 collective-permute-start.25
  291.0 0.3 convolution_bitcast_fusion.4
  291.3 25.1 %collective-permute-done.17 = f32[256,2,256]{2,0,1:T(8,128)S(1)} collective-permute-done((f32[256,2,256]{2,0,1:T(8,128)S(1)}, f32[256,2,256]{2,0,1:T(8,128)S(1)}, u32[]{:S(2)}, u32[]{:S(2)}) %collective-permute-start.17) | collective-permute-done | bytes 524320 | tf_op jit(solution)/shard_map/ppermute | solution.py:12
  316.5 14.6 %collective-permute-done.25 = f32[256,2,256]{2,0,1:T(8,128)S(1)} collective-permute-done((f32[256,2,256]{2,0,1:T(8,128)S(1)}, f32[256,2,256]{2,0,1:T(8,128)S(1)}, u32[]{:S(2)}, u32[]{:S(2)}) %collective-permute-start.25) | collective-permute-done | bytes 524320 | tf_op jit(solution)/shard_map/ppermute | solution.py:12
  331.6 4.9 %collective-permute-start.12 = (bf16[256,2,256]{2,0,1:T(8,128)(2,1)S(1)}, bf16[256,2,256]{2,0,1:T(8,128)(2,1)S(1)}, u32[]{:S(2)}, u32[]{:S(2)}) collective-permute-start(bf16[256,2,256]{2,0,1:T(8,128)(2,1)S(1)} %collective-permute-done.10), channel_id=1, source_target_pairs={{0,4},{4,8},{8,12},{12,16},{16,20},{20,24},{24,28},{28,0},{1,5},{5... | collective-permute-start | bytes 786440 | tf_op jit(solution)/shard_map/ppermute | solution.py:12
  337.1 8.7 %collective-permute-done.18 = f32[256,2,256]{2,0,1:T(8,128)S(1)} collective-permute-done((f32[256,2,256]{2,0,1:T(8,128)S(1)}, f32[256,2,256]{2,0,1:T(8,128)S(1)}, u32[]{:S(2)}, u32[]{:S(2)}) %collective-permute-start.18) | collective-permute-done | bytes 524320 | tf_op jit(solution)/shard_map/ppermute | solution.py:12
  346.0 16.3 %collective-permute-done.26 = f32[256,2,256]{2,0,1:T(8,128)S(1)} collective-permute-done((f32[256,2,256]{2,0,1:T(8,128)S(1)}, f32[256,2,256]{2,0,1:T(8,128)S(1)}, u32[]{:S(2)}, u32[]{:S(2)}) %collective-permute-start.26) | collective-permute-done | bytes 524320 | tf_op jit(solution)/shard_map/ppermute | solution.py:12
  363.0 13.7 %collective-permute-done.12 = bf16[256,2,256]{2,0,1:T(8,128)(2,1)S(1)} collective-permute-done((bf16[256,2,256]{2,0,1:T(8,128)(2,1)S(1)}, bf16[256,2,256]{2,0,1:T(8,128)(2,1)S(1)}, u32[]{:S(2)}, u32[]{:S(2)}) %collective-permute-start.12) | collective-permute-done | bytes 262176 | tf_op jit(solution)/shard_map/ppermute | solution.py:12
  377.0 14.5 %collective-permute-done.19 = f32[256,2,256]{2,0,1:T(8,128)S(1)} collective-permute-done((f32[256,2,256]{2,0,1:T(8,128)S(1)}, f32[256,2,256]{2,0,1:T(8,128)S(1)}, u32[]{:S(2)}, u32[]{:S(2)}) %collective-permute-start.19) | collective-permute-done | bytes 524320 | tf_op jit(solution)/shard_map/ppermute | solution.py:12
  391.6 12.5 %collective-permute-done.27 = f32[256,2,256]{2,0,1:T(8,128)S(1)} collective-permute-done((f32[256,2,256]{2,0,1:T(8,128)S(1)}, f32[256,2,256]{2,0,1:T(8,128)S(1)}, u32[]{:S(2)}, u32[]{:S(2)}) %collective-permute-start.27) | collective-permute-done | bytes 524320 | tf_op jit(solution)/shard_map/ppermute | solution.py:12
  404.8 0.3 convolution_bitcast_fusion.2
  405.1 12.3 %collective-permute-done.20 = f32[256,2,256]{2,0,1:T(8,128)S(1)} collective-permute-done((f32[256,2,256]{2,0,1:T(8,128)S(1)}, f32[256,2,256]{2,0,1:T(8,128)S(1)}, u32[]{:S(2)}, u32[]{:S(2)}) %collective-permute-start.20) | collective-permute-done | bytes 524320 | tf_op jit(solution)/shard_map/ppermute | solution.py:12
  417.6 11.3 %collective-permute-done.28 = f32[256,2,256]{2,0,1:T(8,128)S(1)} collective-permute-done((f32[256,2,256]{2,0,1:T(8,128)S(1)}, f32[256,2,256]{2,0,1:T(8,128)S(1)}, u32[]{:S(2)}, u32[]{:S(2)}) %collective-permute-start.28) | collective-permute-done | bytes 524320 | tf_op jit(solution)/shard_map/ppermute | solution.py:12
  429.0 0.3 convolution_add_fusion.1
  429.3 0.3 fusion.30
  429.6 0.9 copy.238
  430.5 1.9 collective-permute-done.21
  432.5 0.8 copy.239
  433.4 5.7 %collective-permute-done.29 = bf16[256,2,256]{2,0,1:T(8,128)(2,1)S(1)} collective-permute-done((bf16[256,2,256]{2,0,1:T(8,128)(2,1)S(1)}, bf16[256,2,256]{2,0,1:T(8,128)(2,1)S(1)}, u32[]{:S(2)}, u32[]{:S(2)}) %collective-permute-start.29) | collective-permute-done | bytes 262176 | tf_op jit(solution)/shard_map/ppermute | solution.py:12
  439.2 0.8 copy.240
  440.0 1.0 reduce-scatter.4.cloned.1.call-done
  (108 shorter events, 11.8 us)
Async XLA Ops:
  7.2 3.1 copy-start.2
  7.2 3.3 copy-start.8
  7.2 35.5 %all-gather.3.cloned.1.call-start = ((), (), s32[]{:S(2)}) async-start(), calls=%async_computation.1 | async-start | bytes 2621440 | tf_op jit(solution)/shard_map/all_gather | solution.py:92
  7.9 433.0 %reduce-scatter.4.cloned.1.call-start = ((), (), s32[]{:S(2)}) async-start(), calls=%async_computation.2 | async-start | bytes 8519680
  9.0 1.5 copy-start
  57.9 0.9 copy-start.3
  57.9 4.0 copy-start.4
  58.8 5.5 %copy-start.5 = (bf16[1,256,512]{2,1,0:T(8,128)(2,1)S(1)}, bf16[1,256,512]{2,1,0:T(8,128)(2,1)}, u32[]{:S(2)}) copy-start(bf16[1,256,512]{2,1,0:T(8,128)(2,1)} %param.17) | copy-start | bytes 786436
  58.8 5.6 %copy-start.6 = (bf16[1,256,512]{2,1,0:T(8,128)(2,1)S(1)}, bf16[1,256,512]{2,1,0:T(8,128)(2,1)}, u32[]{:S(2)}) copy-start(bf16[1,256,512]{2,1,0:T(8,128)(2,1)} %param.13) | copy-start | bytes 786436
  58.8 5.7 %copy-start.1 = (bf16[1,256,512]{2,1,0:T(8,128)(2,1)S(1)}, bf16[1,256,512]{2,1,0:T(8,128)(2,1)}, u32[]{:S(2)}) copy-start(bf16[1,256,512]{2,1,0:T(8,128)(2,1)} %param.16) | copy-start | bytes 786436
  59.8 5.5 %copy-start.9 = (f32[1,2,256]{2,1,0:T(2,128)S(1)}, f32[1,2,256]{2,1,0:T(2,128)}, u32[]{:S(2)}) copy-start(f32[1,2,256]{2,1,0:T(2,128)} %param.18) | copy-start | bytes 6148
  59.8 94.6 %collective-permute-start.1 = (bf16[256,2,256]{2,0,1:T(8,128)(2,1)}, bf16[256,2,256]{2,0,1:T(8,128)(2,1)}, u32[]{:S(2)}, u32[]{:S(2)}) collective-permute-start(bf16[256,2,256]{2,0,1:T(8,128)(2,1)} %copy.174), channel_id=1, source_target_pairs={{0,4},{4,8},{8,12},{12,16},{16,20},{20,24},{24,28},{28,0},{1,5},{5... | collective-permute-start | bytes 786440 | tf_op jit(solution)/shard_map/ppermute | solution.py:12
  62.9 91.7 %collective-permute-start = (bf16[256,2,256]{2,0,1:T(8,128)(2,1)}, bf16[256,2,256]{2,0,1:T(8,128)(2,1)}, u32[]{:S(2)}, u32[]{:S(2)}) collective-permute-start(bf16[256,2,256]{2,0,1:T(8,128)(2,1)} %copy.172), channel_id=1, source_target_pairs={{0,4},{4,8},{8,12},{12,16},{16,20},{20,24},{24,28},{28,0},{1,5},{5... | collective-permute-start | bytes 786440 | tf_op jit(solution)/shard_map/ppermute | solution.py:12
  65.6 6.0 %copy-start.7 = (bf16[1,256,512]{2,1,0:T(8,128)(2,1)S(1)}, bf16[1,256,512]{2,1,0:T(8,128)(2,1)}, u32[]{:S(2)}) copy-start(bf16[1,256,512]{2,1,0:T(8,128)(2,1)} %param.20) | copy-start | bytes 786436
  67.0 102.8 %collective-permute-start.14 = (f32[256,2,256]{2,0,1:T(8,128)}, f32[256,2,256]{2,0,1:T(8,128)}, u32[]{:S(2)}, u32[]{:S(2)}) collective-permute-start(f32[256,2,256]{2,0,1:T(8,128)} %convolution_bitcast_fusion.17), channel_id=1, source_target_pairs={{0,4},{4,8},{8,12},{12,16},{16,20},{20,24},{24,28},{28,0},{1,5},{5... | collective-permute-start | bytes 1572872 | tf_op jit(solution)/shard_map/ppermute | solution.py:12
  69.2 108.3 %collective-permute-start.22 = (f32[256,2,256]{2,0,1:T(8,128)}, f32[256,2,256]{2,0,1:T(8,128)}, u32[]{:S(2)}, u32[]{:S(2)}) collective-permute-start(f32[256,2,256]{2,0,1:T(8,128)} %convolution_bitcast_fusion.9), channel_id=1, source_target_pairs={{0,4},{4,8},{8,12},{12,16},{16,20},{20,24},{24,28},{28,0},{1,5},{5... | collective-permute-start | bytes 1572872 | tf_op jit(solution)/shard_map/ppermute | solution.py:12
  154.4 15.0 %collective-permute-start.3 = (bf16[256,2,256]{2,0,1:T(8,128)(2,1)}, bf16[256,2,256]{2,0,1:T(8,128)(2,1)S(1)}, u32[]{:S(2)}, u32[]{:S(2)}) collective-permute-start(bf16[256,2,256]{2,0,1:T(8,128)(2,1)} %collective-permute-done.1), channel_id=1, source_target_pairs={{0,4},{4,8},{8,12},{12,16},{16,20},{20,24},{24,28},{28,0},{1,5},{5... | collective-permute-start | bytes 786440 | tf_op jit(solution)/shard_map/ppermute | solution.py:12
  154.5 14.7 %collective-permute-start.2 = (bf16[256,2,256]{2,0,1:T(8,128)(2,1)}, bf16[256,2,256]{2,0,1:T(8,128)(2,1)S(1)}, u32[]{:S(2)}, u32[]{:S(2)}) collective-permute-start(bf16[256,2,256]{2,0,1:T(8,128)(2,1)} %collective-permute-done), channel_id=1, source_target_pairs={{0,4},{4,8},{8,12},{12,16},{16,20},{20,24},{24,28},{28,0},{1,5},{5... | collective-permute-start | bytes 786440 | tf_op jit(solution)/shard_map/ppermute | solution.py:12
  171.4 39.3 %collective-permute-start.15 = (f32[256,2,256]{2,0,1:T(8,128)S(1)}, f32[256,2,256]{2,0,1:T(8,128)S(1)}, u32[]{:S(2)}, u32[]{:S(2)}) collective-permute-start(f32[256,2,256]{2,0,1:T(8,128)S(1)} %fusion.9), channel_id=1, source_target_pairs={{0,4},{4,8},{8,12},{12,16},{16,20},{20,24},{24,28},{28,0},{1,5},{5... | collective-permute-start | bytes 1572872 | tf_op jit(solution)/shard_map/ppermute | solution.py:12
  171.5 37.9 %collective-permute-start.5 = (bf16[256,2,256]{2,0,1:T(8,128)(2,1)S(1)}, bf16[256,2,256]{2,0,1:T(8,128)(2,1)S(1)}, u32[]{:S(2)}, u32[]{:S(2)}) collective-permute-start(bf16[256,2,256]{2,0,1:T(8,128)(2,1)S(1)} %collective-permute-done.3), channel_id=1, source_target_pairs={{0,4},{4,8},{8,12},{12,16},{16,20},{20,24},{24,28},{28,0},{1,5},{5... | collective-permute-start | bytes 786440 | tf_op jit(solution)/shard_map/ppermute | solution.py:12
  171.6 37.5 %collective-permute-start.4 = (bf16[256,2,256]{2,0,1:T(8,128)(2,1)S(1)}, bf16[256,2,256]{2,0,1:T(8,128)(2,1)S(1)}, u32[]{:S(2)}, u32[]{:S(2)}) collective-permute-start(bf16[256,2,256]{2,0,1:T(8,128)(2,1)S(1)} %collective-permute-done.2), channel_id=1, source_target_pairs={{0,4},{4,8},{8,12},{12,16},{16,20},{20,24},{24,28},{28,0},{1,5},{5... | collective-permute-start | bytes 786440 | tf_op jit(solution)/shard_map/ppermute | solution.py:12
  178.9 46.2 %collective-permute-start.23 = (f32[256,2,256]{2,0,1:T(8,128)S(1)}, f32[256,2,256]{2,0,1:T(8,128)S(1)}, u32[]{:S(2)}, u32[]{:S(2)}) collective-permute-start(f32[256,2,256]{2,0,1:T(8,128)S(1)} %fusion.10), channel_id=1, source_target_pairs={{0,4},{4,8},{8,12},{12,16},{16,20},{20,24},{24,28},{28,0},{1,5},{5... | collective-permute-start | bytes 1572872 | tf_op jit(solution)/shard_map/ppermute | solution.py:12
  209.9 29.9 %collective-permute-start.7 = (bf16[256,2,256]{2,0,1:T(8,128)(2,1)S(1)}, bf16[256,2,256]{2,0,1:T(8,128)(2,1)S(1)}, u32[]{:S(2)}, u32[]{:S(2)}) collective-permute-start(bf16[256,2,256]{2,0,1:T(8,128)(2,1)S(1)} %collective-permute-done.5), channel_id=1, source_target_pairs={{0,4},{4,8},{8,12},{12,16},{16,20},{20,24},{24,28},{28,0},{1,5},{5... | collective-permute-start | bytes 786440 | tf_op jit(solution)/shard_map/ppermute | solution.py:12
  210.0 29.3 %collective-permute-start.6 = (bf16[256,2,256]{2,0,1:T(8,128)(2,1)S(1)}, bf16[256,2,256]{2,0,1:T(8,128)(2,1)S(1)}, u32[]{:S(2)}, u32[]{:S(2)}) collective-permute-start(bf16[256,2,256]{2,0,1:T(8,128)(2,1)S(1)} %collective-permute-done.4), channel_id=1, source_target_pairs={{0,4},{4,8},{8,12},{12,16},{16,20},{20,24},{24,28},{28,0},{1,5},{5... | collective-permute-start | bytes 786440 | tf_op jit(solution)/shard_map/ppermute | solution.py:12
  210.8 75.0 %collective-permute-start.16 = (f32[256,2,256]{2,0,1:T(8,128)S(1)}, f32[256,2,256]{2,0,1:T(8,128)S(1)}, u32[]{:S(2)}, u32[]{:S(2)}) collective-permute-start(f32[256,2,256]{2,0,1:T(8,128)S(1)} %add.82), channel_id=1, source_target_pairs={{0,4},{4,8},{8,12},{12,16},{16,20},{20,24},{24,28},{28,0},{1,5},{5... | collective-permute-start | bytes 1572872 | tf_op jit(solution)/shard_map/ppermute | solution.py:12
  225.1 60.8 %collective-permute-start.24 = (f32[256,2,256]{2,0,1:T(8,128)S(1)}, f32[256,2,256]{2,0,1:T(8,128)S(1)}, u32[]{:S(2)}, u32[]{:S(2)}) collective-permute-start(f32[256,2,256]{2,0,1:T(8,128)S(1)} %add.89), channel_id=1, source_target_pairs={{0,4},{4,8},{8,12},{12,16},{16,20},{20,24},{24,28},{28,0},{1,5},{5... | collective-permute-start | bytes 1572872 | tf_op jit(solution)/shard_map/ppermute | solution.py:12
  240.4 37.3 %collective-permute-start.9 = (bf16[256,2,256]{2,0,1:T(8,128)(2,1)S(1)}, bf16[256,2,256]{2,0,1:T(8,128)(2,1)S(1)}, u32[]{:S(2)}, u32[]{:S(2)}) collective-permute-start(bf16[256,2,256]{2,0,1:T(8,128)(2,1)S(1)} %collective-permute-done.7), channel_id=1, source_target_pairs={{0,4},{4,8},{8,12},{12,16},{16,20},{20,24},{24,28},{28,0},{1,5},{5... | collective-permute-start | bytes 786440 | tf_op jit(solution)/shard_map/ppermute | solution.py:12
  240.5 45.0 %collective-permute-start.8 = (bf16[256,2,256]{2,0,1:T(8,128)(2,1)S(1)}, bf16[256,2,256]{2,0,1:T(8,128)(2,1)S(1)}, u32[]{:S(2)}, u32[]{:S(2)}) collective-permute-start(bf16[256,2,256]{2,0,1:T(8,128)(2,1)S(1)} %collective-permute-done.6), channel_id=1, source_target_pairs={{0,4},{4,8},{8,12},{12,16},{16,20},{20,24},{24,28},{28,0},{1,5},{5... | collective-permute-start | bytes 786440 | tf_op jit(solution)/shard_map/ppermute | solution.py:12
  277.7 53.8 %collective-permute-start.11 = (bf16[256,2,256]{2,0,1:T(8,128)(2,1)S(1)}, bf16[256,2,256]{2,0,1:T(8,128)(2,1)S(1)}, u32[]{:S(2)}, u32[]{:S(2)}) collective-permute-start(bf16[256,2,256]{2,0,1:T(8,128)(2,1)S(1)} %collective-permute-done.9), channel_id=1, source_target_pairs={{0,4},{4,8},{8,12},{12,16},{16,20},{20,24},{24,28},{28,0},{1,5},{5... | collective-permute-start | bytes 786440 | tf_op jit(solution)/shard_map/ppermute | solution.py:12
  285.4 46.2 %collective-permute-start.10 = (bf16[256,2,256]{2,0,1:T(8,128)(2,1)S(1)}, bf16[256,2,256]{2,0,1:T(8,128)(2,1)S(1)}, u32[]{:S(2)}, u32[]{:S(2)}) collective-permute-start(bf16[256,2,256]{2,0,1:T(8,128)(2,1)S(1)} %collective-permute-done.8), channel_id=1, source_target_pairs={{0,4},{4,8},{8,12},{12,16},{16,20},{20,24},{24,28},{28,0},{1,5},{5... | collective-permute-start | bytes 786440 | tf_op jit(solution)/shard_map/ppermute | solution.py:12
  285.8 30.5 %collective-permute-start.17 = (f32[256,2,256]{2,0,1:T(8,128)S(1)}, f32[256,2,256]{2,0,1:T(8,128)S(1)}, u32[]{:S(2)}, u32[]{:S(2)}) collective-permute-start(f32[256,2,256]{2,0,1:T(8,128)S(1)} %add.83), channel_id=1, source_target_pairs={{0,4},{4,8},{8,12},{12,16},{16,20},{20,24},{24,28},{28,0},{1,5},{5... | collective-permute-start | bytes 1572872 | tf_op jit(solution)/shard_map/ppermute | solution.py:12
  286.0 45.1 %collective-permute-start.25 = (f32[256,2,256]{2,0,1:T(8,128)S(1)}, f32[256,2,256]{2,0,1:T(8,128)S(1)}, u32[]{:S(2)}, u32[]{:S(2)}) collective-permute-start(f32[256,2,256]{2,0,1:T(8,128)S(1)} %add.90), channel_id=1, source_target_pairs={{0,4},{4,8},{8,12},{12,16},{16,20},{20,24},{24,28},{28,0},{1,5},{5... | collective-permute-start | bytes 1572872 | tf_op jit(solution)/shard_map/ppermute | solution.py:12
  316.4 29.4 %collective-permute-start.18 = (f32[256,2,256]{2,0,1:T(8,128)S(1)}, f32[256,2,256]{2,0,1:T(8,128)S(1)}, u32[]{:S(2)}, u32[]{:S(2)}) collective-permute-start(f32[256,2,256]{2,0,1:T(8,128)S(1)} %add.84), channel_id=1, source_target_pairs={{0,4},{4,8},{8,12},{12,16},{16,20},{20,24},{24,28},{28,0},{1,5},{5... | collective-permute-start | bytes 1572872 | tf_op jit(solution)/shard_map/ppermute | solution.py:12
  331.2 31.2 %collective-permute-start.26 = (f32[256,2,256]{2,0,1:T(8,128)S(1)}, f32[256,2,256]{2,0,1:T(8,128)S(1)}, u32[]{:S(2)}, u32[]{:S(2)}) collective-permute-start(f32[256,2,256]{2,0,1:T(8,128)S(1)} %add.91), channel_id=1, source_target_pairs={{0,4},{4,8},{8,12},{12,16},{16,20},{20,24},{24,28},{28,0},{1,5},{5... | collective-permute-start | bytes 1572872 | tf_op jit(solution)/shard_map/ppermute | solution.py:12
  331.5 72.7 %collective-permute-start.13 = (bf16[256,2,256]{2,0,1:T(8,128)(2,1)S(1)}, bf16[256,2,256]{2,0,1:T(8,128)(2,1)S(1)}, u32[]{:S(2)}, u32[]{:S(2)}) collective-permute-start(bf16[256,2,256]{2,0,1:T(8,128)(2,1)S(1)} %collective-permute-done.11), channel_id=1, source_target_pairs={{0,4},{4,8},{8,12},{12,16},{16,20},{20,24},{24,28},{28,0},{1,5},{5... | collective-permute-start | bytes 786440 | tf_op jit(solution)/shard_map/ppermute | solution.py:12
  331.6 45.1 %collective-permute-start.12 = (bf16[256,2,256]{2,0,1:T(8,128)(2,1)S(1)}, bf16[256,2,256]{2,0,1:T(8,128)(2,1)S(1)}, u32[]{:S(2)}, u32[]{:S(2)}) collective-permute-start(bf16[256,2,256]{2,0,1:T(8,128)(2,1)S(1)} %collective-permute-done.10), channel_id=1, source_target_pairs={{0,4},{4,8},{8,12},{12,16},{16,20},{20,24},{24,28},{28,0},{1,5},{5... | collective-permute-start | bytes 786440 | tf_op jit(solution)/shard_map/ppermute | solution.py:12
  345.9 45.6 %collective-permute-start.19 = (f32[256,2,256]{2,0,1:T(8,128)S(1)}, f32[256,2,256]{2,0,1:T(8,128)S(1)}, u32[]{:S(2)}, u32[]{:S(2)}) collective-permute-start(f32[256,2,256]{2,0,1:T(8,128)S(1)} %add.85), channel_id=1, source_target_pairs={{0,4},{4,8},{8,12},{12,16},{16,20},{20,24},{24,28},{28,0},{1,5},{5... | collective-permute-start | bytes 1572872 | tf_op jit(solution)/shard_map/ppermute | solution.py:12
  362.4 41.7 %collective-permute-start.27 = (f32[256,2,256]{2,0,1:T(8,128)S(1)}, f32[256,2,256]{2,0,1:T(8,128)S(1)}, u32[]{:S(2)}, u32[]{:S(2)}) collective-permute-start(f32[256,2,256]{2,0,1:T(8,128)S(1)} %add.92), channel_id=1, source_target_pairs={{0,4},{4,8},{8,12},{12,16},{16,20},{20,24},{24,28},{28,0},{1,5},{5... | collective-permute-start | bytes 1572872 | tf_op jit(solution)/shard_map/ppermute | solution.py:12
  391.5 25.9 %collective-permute-start.20 = (f32[256,2,256]{2,0,1:T(8,128)S(1)}, f32[256,2,256]{2,0,1:T(8,128)S(1)}, u32[]{:S(2)}, u32[]{:S(2)}) collective-permute-start(f32[256,2,256]{2,0,1:T(8,128)S(1)} %add.86), channel_id=1, source_target_pairs={{0,4},{4,8},{8,12},{12,16},{16,20},{20,24},{24,28},{28,0},{1,5},{5... | collective-permute-start | bytes 1572872 | tf_op jit(solution)/shard_map/ppermute | solution.py:12
  404.2 24.7 %collective-permute-start.28 = (f32[256,2,256]{2,0,1:T(8,128)S(1)}, f32[256,2,256]{2,0,1:T(8,128)S(1)}, u32[]{:S(2)}, u32[]{:S(2)}) collective-permute-start(f32[256,2,256]{2,0,1:T(8,128)S(1)} %add.93), channel_id=1, source_target_pairs={{0,4},{4,8},{8,12},{12,16},{16,20},{20,24},{24,28},{28,0},{1,5},{5... | collective-permute-start | bytes 1572872 | tf_op jit(solution)/shard_map/ppermute | solution.py:12
  417.5 14.9 %collective-permute-start.21 = (bf16[256,2,256]{2,0,1:T(8,128)(2,1)S(1)}, bf16[256,2,256]{2,0,1:T(8,128)(2,1)S(1)}, u32[]{:S(2)}, u32[]{:S(2)}) collective-permute-start(bf16[256,2,256]{2,0,1:T(8,128)(2,1)S(1)} %add.87), channel_id=1, source_target_pairs={{0,4},{4,8},{8,12},{12,16},{16,20},{20,24},{24,28},{28,0},{1,5},{5... | collective-permute-start | bytes 786440 | tf_op jit(solution)/shard_map/ppermute | solution.py:12
  429.0 10.1 %collective-permute-start.29 = (bf16[256,2,256]{2,0,1:T(8,128)(2,1)S(1)}, bf16[256,2,256]{2,0,1:T(8,128)(2,1)S(1)}, u32[]{:S(2)}, u32[]{:S(2)}) collective-permute-start(bf16[256,2,256]{2,0,1:T(8,128)(2,1)S(1)} %add.94), channel_id=1, source_target_pairs={{0,4},{4,8},{8,12},{12,16},{16,20},{20,24},{24,28},{28,0},{1,5},{5... | collective-permute-start | bytes 786440 | tf_op jit(solution)/shard_map/ppermute | solution.py:12
Sparse Core Ops, SparseCore 0:
  9.8 32.8 all-gather.2
  58.0 382.8 reduce-scatter.3
where the time goes:
time: 457 us; the launch traced here: 448 us
  waiting for transfers between devices  270 us (59%)
  blocking collectives  76.4 us (17%)
  starting transfers between devices  37.7 us (8%)
  matrix products  25.9 us (6%)
  local copies, waits for them, and re-layouts  21.8 us (5%)
  between operations  15.1 us (3%)
    ppermute x30, waiting for transfers between devices, passed_along(): return lax.ppermute(value, axis, pairs)  236 us
    psum x1, blocking collectives, body(): summary_total = lax.psum(summary_part, 'blk')  76.4 us
    ppermute x30, starting transfers between devices, passed_along(): return lax.ppermute(value, axis, pairs)  37.6 us
    all_gather x1, waiting for transfers between devices, body(): states_all = lax.all_gather(encoder_states[0], 'mp', axis=1, tiled=True)  31.7 us
    unnamed x29, local copies, waits for them, and re-layouts  15.4 us
  transfers between devices with their start and end apart: 32, of which 19 were waited for; matrix products, arithmetic and copies ran while one was open for 7% of the time, Pallas kernels for 0%

commit v1 on v0

v1 whole, which is shorter than its diff:
```python
import jax
import jax.numpy as jnp
from jax import lax
from jax.experimental import pallas as pl
from jax.experimental.pallas import tpu as pltpu
from jax.sharding import PartitionSpec as P

HD = 256
NX = 4
NZ = 8
F32 = jnp.float32
BF16 = jnp.bfloat16
MESH = pl.DeviceIdType.MESH
ORDER = (0, 1, 3, 2)


def mm(a, b, ca, cb):
    return lax.dot_general(a, b, (((ca,), (cb,)), ((), ())), preferred_element_type=F32)


def row_sums(grad, out):
    product = grad.astype(F32) * out.astype(F32)
    high = product.astype(BF16)
    low = (product - high.astype(F32)).astype(BF16)
    ones = jnp.ones((8, HD), BF16)
    return mm(ones, high, 1, 1) + mm(ones, low, 1, 1)


def remote(src, dst, send, recv, device):
    return pltpu.make_async_remote_copy(
        src_ref=src, dst_ref=dst, send_sem=send, recv_sem=recv, device_id=device, device_id_type=MESH
    )


def arrived(dst, sem):
    pltpu.make_async_copy(dst, dst, sem).wait()


def push(src, dst, send, recv, device, here):
    @pl.when(here)
    def _():
        pltpu.make_async_copy(src, dst, recv).start()

    @pl.when(jnp.logical_not(here))
    def _():
        remote(src, dst, send, recv, device).start()


def pushed(src, dst, send, recv, device, here):
    @pl.when(jnp.logical_not(here))
    def _():
        remote(src, dst, send, recv, device).wait_send()


def kernel(
    eq, ek, ev, eo, ed, et, ck, cv, dq, do, dd, dt, es,
    out_q, out_k, out_v, out_ck, out_cv, out_dq, out_w,
    st_src, st_all, vg_all, z_src, z_recv, y_src, y_recv,
    kv, qd, stats_src, stats, acc, acc_recv, fin, dq_own, dq_send, dq_recv, dq_fin, raw,
    dec_src, dec_recv, dec_mine, dec_other, dec_all,
    st_s, st_r, sty_s, stc_s, vg_s, vg_r, z_s, z_r, y_s, y_r,
    kv_s, kv_r, kvc_s, qd_s, qd_r, qdy_s, sta_s, sta_r, stay_s,
    acc_s, acc_r, fin_s, raw_r, dqy_s, dqy_r, dqo_s,
    dec_s, dec_r, decy_s, decy_r, deca_s, deca_r,
):
    z = lax.axis_index("dp")
    blk = lax.axis_index("blk")
    mp = lax.axis_index("mp")
    yh, x = blk // NX, blk % NX
    yl, c = mp // 2, mp % 2
    oyh, oyl, oc = 1 - yh, 1 - yl, 1 - c

    def dev(z_=None, yh_=None, x_=None, yl_=None, c_=None):
        z_ = z if z_ is None else z_
        yh_ = yh if yh_ is None else yh_
        x_ = x if x_ is None else x_
        yl_ = yl if yl_ is None else yl_
        c_ = c if c_ is None else c_
        return (z_, yh_ * NX + x_, yl_ * 2 + c_)

    def at_x(d):
        return (x + d) % NX

    sibling = dev(c_=oc)
    ylo = dev(yl_=oyl)
    yhi = dev(yh_=oyh)

    barrier = pltpu.get_barrier_semaphore()
    partners = [dev(x_=at_x(d), c_=(c + dc) % 2) for d in range(NX) for dc in range(2) if d or dc]
    partners += [yhi, ylo]
    partners += [dev(z_=(z + d) % NZ) for d in range(1, NZ)]
    for partner in partners:
        pl.semaphore_signal(barrier, inc=1, device_id=partner, device_id_type=MESH)

    for k in range(4):
        piece = es[0, :, k * 256:(k + 1) * 256].T
        st_src[k] = piece.reshape(NX, 64, 256)
    st_all[mp, x] = st_src[:, x]

    for e in range(2):
        cols = slice(e * HD, (e + 1) * HD)
        keys, vals = ck[0, :, cols], cv[0, :, cols]
        query, grad = dq[0, :, cols], dd[0, :, cols]
        inv = 1.0 / dt[0, e:e + 1, :]
        delta = row_sums(grad, do[0, :, cols])[0:1, :]
        probs = jnp.exp(mm(keys, query, 1, 1)) * inv
        weights = probs.astype(BF16)
        dscores = (probs * (mm(vals, grad, 1, 1) - delta)).astype(BF16)
        value_grad = mm(weights, grad, 1, 0).astype(BF16)
        out_cv[0, :, cols] = value_grad
        vg_all[x, :, cols] = value_grad
        out_ck[0, :, cols] = mm(dscores, query, 1, 0).astype(BF16)
        part = mm(dscores, keys, 0, 0).astype(BF16)
        dec_src[:, :, cols] = part.reshape(NX, 64, HD)
        stats_src[e, 0:4, :] = jnp.broadcast_to(1.0 / et[0, e:e + 1, :], (4, 256))
        stats_src[e, 4:8, :] = row_sums(ed[0, :, cols], eo[0, :, cols])[0:4, :]
    dec_recv[x] = dec_src[x]

    pl.semaphore_wait(barrier, len(partners))

    st_out = [remote(st_src.at[:, at_x(d)], st_all.at[mp, x], st_s.at[d], st_r.at[mp, x], dev(x_=at_x(d)))
              for d in (1, 3, 2)]
    vg_out = [remote(vg_all.at[x], vg_all.at[x], vg_s.at[d], vg_r.at[x], dev(x_=at_x(d))) for d in (1, 3, 2)]
    dec_out = [remote(dec_src.at[at_x(d)], dec_recv.at[x], dec_s.at[d], dec_r.at[x], dev(x_=at_x(d)))
               for d in (1, 3, 2)]
    for cp in st_out:
        cp.start()

    def st_to_ylo(s):
        return remote(st_all.at[mp, s], st_all.at[mp, s], sty_s.at[s], st_r.at[mp, s], ylo)

    def st_to_sibling(m, k, s):
        return remote(st_all.at[m, s], st_all.at[m, s], stc_s.at[k, s], st_r.at[m, s], sibling)

    mine, other = mp, oyl * 2 + c
    st_to_ylo(x).start()
    st_to_sibling(mine, 0, x).start()
    for cp in vg_out:
        cp.start()

    enc_out = []
    for i in range(2):
        e = (x + i) % 2
        xt = 2 * c + e
        cols = pl.ds(pl.multiple_of(e * HD, HD), HD)
        for a, src in ((0, ek), (1, ev)):
            enc_out.append((src.at[0, :, cols], kv.at[a, x], kv_s.at[i, a], kv_r.at[a, x],
                            dev(x_=xt, c_=a), jnp.logical_and(xt == x, c == a)))
        here = jnp.logical_and(xt == x, c == yh)
        target = dev(x_=xt, c_=yh)
        for a, src in ((0, eq), (1, ed)):
            enc_out.append((src.at[0, :, cols], qd.at[x, a], qd_s.at[i, a], qd_r.at[x, a], target, here))
        enc_out.append((stats_src.at[e], stats.at[x], sta_s.at[i], sta_r.at[x], target, here))
    for args in enc_out:
        push(*args)
    for cp in dec_out:
        cp.start()

    for d in (1, 3, 2):
        s = at_x(d)
        arrived(st_all.at[mine, s], st_r.at[mine, s])
        st_to_ylo(s).start()
        st_to_sibling(mine, 0, s).start()
    for d in ORDER:
        s = at_x(d)
        arrived(st_all.at[other, s], st_r.at[other, s])
        st_to_sibling(other, 1, s).start()

    for d in (1, 3, 2):
        s = at_x(d)
        arrived(dec_recv.at[s], dec_r.at[s])
    total = dec_recv[0].astype(F32)
    for s in range(1, NX):
        total = total + dec_recv[s].astype(F32)
    dec_mine[...] = total
    dec_swap = remote(dec_mine, dec_other, decy_s, decy_r, yhi)
    dec_swap.start()

    def kv_to_sibling(s):
        return remote(kv.at[c, s], kv.at[c, s], kvc_s.at[s], kv_r.at[c, s], sibling)

    def qd_to_yhi(s):
        return [remote(qd.at[s, a], qd.at[s, a], qdy_s.at[s, a], qd_r.at[s, a], yhi) for a in range(2)] + [
            remote(stats.at[s], stats.at[s], stay_s.at[s], sta_r.at[s], yhi)]

    def qd_arrived(s):
        for a in range(2):
            arrived(qd.at[s, a], qd_r.at[s, a])
        arrived(stats.at[s], sta_r.at[s])

    first_hand = c == yh
    for d in ORDER:
        s = at_x(d)
        arrived(kv.at[c, s], kv_r.at[c, s])
        kv_to_sibling(s).start()

        @pl.when(first_hand)
        def _(s=s):
            qd_arrived(s)
            for cp in qd_to_yhi(s):
                cp.start()

    for d in (1, 3, 2):
        s = at_x(d)
        arrived(vg_all.at[s], vg_r.at[s])
    for s in range(NX):
        arrived(st_all.at[yl * 2 + oc, s], st_r.at[yl * 2 + oc, s])
        arrived(st_all.at[oyl * 2 + oc, s], st_r.at[oyl * 2 + oc, s])

    z_out = []
    for k in range(4):
        m = (z // 2 + k) % 4
        part = mm(st_all[m, 0].reshape(256, 256), vg_all[0], 1, 0)
        for s in range(1, NX):
            part = part + mm(st_all[m, s].reshape(256, 256), vg_all[s], 1, 0)
        z_src[k] = part.astype(BF16).reshape(2, 128, 512)
        for l in range(2):
            zt = 2 * m + l
            args = (z_src.at[k, l], z_recv.at[z], z_s.at[k, l], z_r.at[z], dev(z_=zt), zt == z)
            push(*args)
            z_out.append(args)

    dec_swap.wait()
    dec_all[x] = (dec_mine[...] + dec_other[...]).astype(BF16)
    deca_out = [remote(dec_all.at[x], dec_all.at[x], deca_s.at[d], deca_r.at[x], dev(x_=at_x(d))) for d in (1, 3, 2)]
    for cp in deca_out:
        cp.start()

    for s in range(NX):
        arrived(kv.at[oc, s], kv_r.at[oc, s])

    def dq_to_yhi(s):
        return remote(dq_send.at[s], dq_recv.at[s], dqy_s.at[s], dqy_r.at[s], yhi)

    def acc_to_sibling(b):
        return remote(acc.at[oc, b], acc_recv.at[b], acc_s.at[b], acc_r.at[b], sibling)

    for i, d in enumerate(ORDER):
        s = at_x(d)

        @pl.when(jnp.logical_not(first_hand))
        def _(s=s):
            qd_arrived(s)

        query, grad = qd[s, 0], qd[s, 1]
        inv, delta = stats[s, 0:1, :], stats[s, 4:5, :]
        grad_q = jnp.zeros((256, HD), F32)
        for h in range(2):
            keys = kv[0, 2 * h:2 * h + 2].reshape(512, HD)
            vals = kv[1, 2 * h:2 * h + 2].reshape(512, HD)
            probs = jnp.exp(mm(keys, query, 1, 1)) * inv
            weights = probs.astype(BF16)
            dscores = (probs * (mm(vals, grad, 1, 1) - delta)).astype(BF16)
            value_part = mm(weights, grad, 1, 0).reshape(2, 256, HD)
            key_part = mm(dscores, query, 1, 0).reshape(2, 256, HD)
            grad_q = grad_q + mm(dscores, keys, 0, 0)
            if i:
                key_part = key_part + acc[0, 2 * h:2 * h + 2]
                value_part = value_part + acc[1, 2 * h:2 * h + 2]
            acc[0, 2 * h:2 * h + 2] = key_part
            acc[1, 2 * h:2 * h + 2] = value_part
            if i == NX - 1:
                for b in (2 * h, 2 * h + 1):
                    acc_to_sibling(b).start()

        @pl.when(first_hand)
        def _(s=s, grad_q=grad_q):
            dq_own[s] = grad_q

        @pl.when(jnp.logical_not(first_hand))
        def _(s=s, grad_q=grad_q):
            dq_send[s] = grad_q.astype(BF16)
            dq_to_yhi(s).start()

    e_of = x % 2
    owner_c = x // 2
    fin_out = []
    for b in range(NX):
        arrived(acc_recv.at[b], acc_r.at[b])
        fin[b] = (acc[c, b] + acc_recv[b]).astype(BF16)
        args = (fin.at[b], raw.at[c, e_of], fin_s.at[b], raw_r.at[c, e_of], dev(x_=b, c_=owner_c),
                jnp.logical_and(b == x, c == owner_c))
        push(*args)
        fin_out.append(args)

    def dq_args(s):
        return (dq_fin.at[s], raw.at[2, e_of], dqo_s.at[s], raw_r.at[2, e_of], dev(x_=s, c_=owner_c),
                jnp.logical_and(s == x, c == owner_c))

    @pl.when(first_hand)
    def _():
        for d in ORDER:
            s = at_x(d)
            arrived(dq_recv.at[s], dqy_r.at[s])
            dq_fin[s] = (dq_own[s] + dq_recv[s].astype(F32)).astype(BF16)
            push(*dq_args(s))

    for s in range(NZ):
        arrived(z_recv.at[s], z_r.at[s])
    w = z_recv[0].astype(F32)
    for s in range(1, NZ):
        w = w + z_recv[s].astype(F32)
    y_src[...] = w.reshape(2, 64, 512)
    y_swap = remote(y_src.at[oyh], y_recv, y_s, y_r, yhi)
    y_swap.start()

    for d in (1, 3, 2):
        s = at_x(d)
        arrived(dec_all.at[s], deca_r.at[s])
    out_dq[0] = dec_all[...].reshape(256, 512)

    for e in range(2):
        cols = slice(e * HD, (e + 1) * HD)
        for a, out in ((0, out_k), (1, out_v), (2, out_q)):
            arrived(raw.at[a, e], raw_r.at[a, e])
            out[0, :, cols] = raw[a, e]

    y_swap.wait()
    out_w[...] = y_src[yh] + y_recv[...]

    for cp in st_out + vg_out + dec_out + deca_out:
        cp.wait_send()
    for d in range(NX):
        st_to_ylo(d).wait_send()
        st_to_sibling(mine, 0, d).wait_send()
        st_to_sibling(other, 1, d).wait_send()
        kv_to_sibling(d).wait_send()
        acc_to_sibling(d).wait_send()
    for args in enc_out + z_out + fin_out:
        pushed(*args)

    @pl.when(first_hand)
    def _():
        for s in range(NX):
            for cp in qd_to_yhi(s):
                cp.wait_send()
            pushed(*dq_args(s))

    @pl.when(jnp.logical_not(first_hand))
    def _():
        for s in range(NX):
            dq_to_yhi(s).wait_send()


def body(*arrays):
    vmem = pl.BlockSpec(memory_space=pltpu.VMEM)
    dma = pltpu.SemaphoreType.DMA
    outs = [jax.ShapeDtypeStruct((1, 256, 512), BF16) for _ in range(6)]
    outs.append(jax.ShapeDtypeStruct((64, 512), F32))
    buffers = [
        ((4, NX, 64, 256), BF16), ((4, NX, 4, 64, 256), BF16), ((NX, 256, 512), BF16),
        ((4, 2, 128, 512), BF16), ((NZ, 128, 512), BF16), ((2, 64, 512), F32), ((64, 512), F32),
        ((2, NX, 256, HD), BF16), ((NX, 2, 256, HD), BF16), ((2, 8, 256), F32), ((NX, 8, 256), F32),
        ((2, NX, 256, HD), F32), ((NX, 256, HD), F32), ((NX, 256, HD), BF16), ((NX, 256, HD), F32),
        ((NX, 256, HD), BF16), ((NX, 256, HD), BF16), ((NX, 256, HD), BF16), ((3, 2, 256, HD), BF16),
        ((NX, 64, 512), BF16), ((NX, 64, 512), BF16), ((64, 512), F32), ((64, 512), F32), ((NX, 64, 512), BF16),
    ]
    semaphores = [
        (NX,), (4, NX), (NX,), (2, NX), (NX,), (NX,), (4, 2), (NZ,), None, None,
        (2, 2), (2, NX), (NX,), (2, 2), (NX, 2), (NX, 2), (2,), (NX,), (NX,),
        (NX,), (NX,), (NX,), (3, 2), (NX,), (NX,), (NX,),
        (NX,), (NX,), None, None, (NX,), (NX,),
    ]
    scratch = [pltpu.VMEM(shape, dtype) for shape, dtype in buffers]
    scratch += [dma if shape is None else dma(shape) for shape in semaphores]
    return tuple(pl.pallas_call(
        kernel,
        out_shape=outs,
        in_specs=[vmem] * 13,
        out_specs=[vmem] * 7,
        scratch_shapes=scratch,
        compiler_params=pltpu.CompilerParams(
            collective_id=0, has_side_effects=True, vmem_limit_bytes=48 * 1024 * 1024
        ),
        cost_estimate=pl.CostEstimate(flops=5_000_000_000, bytes_accessed=6_000_000, transcendentals=1_200_000),
        name="grads",
    )(*arrays))


def solution(mesh):
    rows = P("dp", "blk", "mp")
    tokens = P("dp", None, "mp")
    in_specs = (rows, rows, rows, rows, rows, P("dp", "mp", "blk"), rows, rows, tokens, tokens, tokens,
                P("dp", "mp", None), rows)
    out_specs = (rows, rows, rows, rows, rows, tokens, P(("dp", "blk"), "mp"))
    return jax.shard_map(body, mesh=mesh, in_specs=in_specs, out_specs=out_specs, check_vma=False)
```

time: 457 us -> 95.3 us (0.21)
  the two profiles are of different devices: /device:TPU:8 before, /device:TPU:1 now
where the time goes in v1:
time: 95.3 us; the launch traced here: 94.9 us
  Pallas kernels  77.4 us (81%)
  local copies, waits for them, and re-layouts  16.8 us (18%)
    pallas_call x1, Pallas kernels, body(): pl.pallas_call(kernel, out_shape=outs, in_specs=[vmem] * 13, out_specs=[v...  77.4 us
    unnamed x33, local copies, waits for them, and re-layouts  16.8 us

profile of v1, /device:TPU:1, one launch (start us, length us, event | category | flops | bytes accessed | tf_op | source)
XLA Modules:
  0.0 94.9 jit_solution(394051556654606698)
XLA Ops:
  0.6 0.0 copy-start
  0.6 1.0 %copy-done = bf16[1,256,1024]{2,1,0:T(8,128)(2,1)S(1)} copy-done((bf16[1,256,1024]{2,1,0:T(8,128)(2,1)S(1)}, bf16[1,256,1024]{2,1,0:T(8,128)(2,1)}, u32[]{:S(2)}) %copy-start) | copy-done | bytes 524312
  1.7 0.0 copy-start.1
  1.7 0.9 copy-done.1
  2.6 0.0 copy-start.2
  2.6 0.9 copy-done.2
  3.6 0.0 copy-start.3
  3.6 0.9 copy-done.3
  4.5 0.0 copy-start.4
  4.5 0.9 copy-done.4
  5.5 0.0 copy-start.5
  5.5 0.9 copy-done.5
  6.4 0.0 copy-start.6
  6.4 0.9 copy-done.6
  7.4 0.0 copy-start.7
  7.4 0.9 copy-done.7
  8.3 0.0 copy-start.8
  8.3 0.9 copy-done.8
  9.3 0.0 copy-start.9
  9.3 0.9 copy-done.9
  10.2 0.0 copy-start.10
  10.2 0.9 copy-done.10
  11.2 0.0 copy-start.11
  11.2 0.7 copy-done.11
  11.9 0.0 copy-start.12
  11.9 0.7 copy-done.12
  12.6 77.4 %grads.1 = (bf16[1,256,512]{2,1,0:T(8,128)(2,1)S(1)}, bf16[1,256,512]{2,1,0:T(8,128)(2,1)S(1)}, bf16[1,256,512]{2,1,0:T(8,128)(2,1)S(1)}, bf16[1,256,512]{2,1,0:...) custom-call(bf16[1,256,512]{2,1,0:T(8,128)(2,1)S(1)} %copy-done.1, ...), custom_call_target="tpu_custom_call" | custom-call | flops 5000000000 | bytes 6000000 | tf_op jit(solution)/shard_map/grads/pallas_call | solution.py:366
  90.0 0.7 copy.27
  90.7 0.7 copy.28
  91.4 0.7 copy.29
  92.1 0.7 copy.30
  92.8 0.7 copy.31
  93.5 0.7 copy.32
  94.2 0.7 copy.33
Async XLA Ops:
  0.6 1.0 %copy-start = (bf16[1,256,1024]{2,1,0:T(8,128)(2,1)S(1)}, bf16[1,256,1024]{2,1,0:T(8,128)(2,1)}, u32[]{:S(2)}) copy-start(bf16[1,256,1024]{2,1,0:T(8,128)(2,1)} %es.1) | copy-start | bytes 1572868
  1.7 0.9 %copy-start.1 = (bf16[1,256,512]{2,1,0:T(8,128)(2,1)S(1)}, bf16[1,256,512]{2,1,0:T(8,128)(2,1)}, u32[]{:S(2)}) copy-start(bf16[1,256,512]{2,1,0:T(8,128)(2,1)} %eq.1) | copy-start | bytes 786436
  2.6 0.9 %copy-start.2 = (bf16[1,256,512]{2,1,0:T(8,128)(2,1)S(1)}, bf16[1,256,512]{2,1,0:T(8,128)(2,1)}, u32[]{:S(2)}) copy-start(bf16[1,256,512]{2,1,0:T(8,128)(2,1)} %ek.1) | copy-start | bytes 786436
  3.6 0.9 %copy-start.3 = (bf16[1,256,512]{2,1,0:T(8,128)(2,1)S(1)}, bf16[1,256,512]{2,1,0:T(8,128)(2,1)}, u32[]{:S(2)}) copy-start(bf16[1,256,512]{2,1,0:T(8,128)(2,1)} %ev.1) | copy-start | bytes 786436
  4.5 0.9 %copy-start.4 = (bf16[1,256,512]{2,1,0:T(8,128)(2,1)S(1)}, bf16[1,256,512]{2,1,0:T(8,128)(2,1)}, u32[]{:S(2)}) copy-start(bf16[1,256,512]{2,1,0:T(8,128)(2,1)} %eo.1) | copy-start | bytes 786436
  5.5 0.9 %copy-start.5 = (bf16[1,256,512]{2,1,0:T(8,128)(2,1)S(1)}, bf16[1,256,512]{2,1,0:T(8,128)(2,1)}, u32[]{:S(2)}) copy-start(bf16[1,256,512]{2,1,0:T(8,128)(2,1)} %ed.1) | copy-start | bytes 786436
  6.4 0.9 %copy-start.6 = (bf16[1,256,512]{2,1,0:T(8,128)(2,1)S(1)}, bf16[1,256,512]{2,1,0:T(8,128)(2,1)}, u32[]{:S(2)}) copy-start(bf16[1,256,512]{2,1,0:T(8,128)(2,1)} %ck.1) | copy-start | bytes 786436
  7.4 0.9 %copy-start.7 = (bf16[1,256,512]{2,1,0:T(8,128)(2,1)S(1)}, bf16[1,256,512]{2,1,0:T(8,128)(2,1)}, u32[]{:S(2)}) copy-start(bf16[1,256,512]{2,1,0:T(8,128)(2,1)} %cv.1) | copy-start | bytes 786436
  8.3 0.9 %copy-start.8 = (bf16[1,256,512]{2,1,0:T(8,128)(2,1)S(1)}, bf16[1,256,512]{2,1,0:T(8,128)(2,1)}, u32[]{:S(2)}) copy-start(bf16[1,256,512]{2,1,0:T(8,128)(2,1)} %dq.1) | copy-start | bytes 786436
  9.3 0.9 %copy-start.9 = (bf16[1,256,512]{2,1,0:T(8,128)(2,1)S(1)}, bf16[1,256,512]{2,1,0:T(8,128)(2,1)}, u32[]{:S(2)}) copy-start(bf16[1,256,512]{2,1,0:T(8,128)(2,1)} %do.1) | copy-start | bytes 786436
  10.2 0.9 %copy-start.10 = (bf16[1,256,512]{2,1,0:T(8,128)(2,1)S(1)}, bf16[1,256,512]{2,1,0:T(8,128)(2,1)}, u32[]{:S(2)}) copy-start(bf16[1,256,512]{2,1,0:T(8,128)(2,1)} %dd.1) | copy-start | bytes 786436
  11.2 0.7 copy-start.11
  11.9 0.7 copy-start.12

commit v2 on v1

--- a/solution.py
+++ b/solution.py
@@ -12,6 +12,10 @@
 BF16 = jnp.bfloat16
 MESH = pl.DeviceIdType.MESH
 ORDER = (0, 1, 3, 2)
+RELAY = False
+GATE = 0
+SWAP = F32
+PLAN = 1
 
 
 def mm(a, b, ca, cb):
@@ -54,9 +58,10 @@
 
 def kernel(
     eq, ek, ev, eo, ed, et, ck, cv, dq, do, dd, dt, es,
-    out_q, out_k, out_v, out_ck, out_cv, out_dq, out_w,
-    st_src, st_all, vg_all, z_src, z_recv, y_src, y_recv,
-    kv, qd, stats_src, stats, acc, acc_recv, fin, dq_own, dq_send, dq_recv, dq_fin, raw,
+    raw, out_ck, out_cv, out_dq, out_w,
+    es_v, ck_v, cv_v, dq_v, do_v, dd_v, dt_v, eo_v, ed_v, et_v, load_s,
+    st_src, st_all, vg_all, z_src, z_recv, y_own, y_src, y_recv,
+    kv, qd, stats_src, stats, acc, acc_recv, fin, dq_own, dq_send, dq_recv, dq_fin,
     dec_src, dec_recv, dec_mine, dec_other, dec_all,
     st_s, st_r, sty_s, stc_s, vg_s, vg_r, z_s, z_r, y_s, y_r,
     kv_s, kv_r, kvc_s, qd_s, qd_r, qdy_s, sta_s, sta_r, stay_s,
@@ -92,35 +97,26 @@
     for partner in partners:
         pl.semaphore_signal(barrier, inc=1, device_id=partner, device_id_type=MESH)
 
+    loads = [pltpu.make_async_copy(src, dst, load_s.at[i]) for i, (src, dst) in enumerate(
+        ((es, es_v), (ck, ck_v), (dq, dq_v), (dt, dt_v), (dd, dd_v), (cv, cv_v), (do, do_v),
+         (eo, eo_v), (ed, ed_v), (et, et_v)))]
+    for cp in loads:
+        cp.start()
+
+    loads[0].wait()
     for k in range(4):
-        piece = es[0, :, k * 256:(k + 1) * 256].T
+        piece = es_v[0, :, k * 256:(k + 1) * 256].T
         st_src[k] = piece.reshape(NX, 64, 256)
     st_all[mp, x] = st_src[:, x]
 
-    for e in range(2):
-        cols = slice(e * HD, (e + 1) * HD)
-        keys, vals = ck[0, :, cols], cv[0, :, cols]
-        query, grad = dq[0, :, cols], dd[0, :, cols]
-        inv = 1.0 / dt[0, e:e + 1, :]
-        delta = row_sums(grad, do[0, :, cols])[0:1, :]
-        probs = jnp.exp(mm(keys, query, 1, 1)) * inv
-        weights = probs.astype(BF16)
-        dscores = (probs * (mm(vals, grad, 1, 1) - delta)).astype(BF16)
-        value_grad = mm(weights, grad, 1, 0).astype(BF16)
-        out_cv[0, :, cols] = value_grad
-        vg_all[x, :, cols] = value_grad
-        out_ck[0, :, cols] = mm(dscores, query, 1, 0).astype(BF16)
-        part = mm(dscores, keys, 0, 0).astype(BF16)
-        dec_src[:, :, cols] = part.reshape(NX, 64, HD)
-        stats_src[e, 0:4, :] = jnp.broadcast_to(1.0 / et[0, e:e + 1, :], (4, 256))
-        stats_src[e, 4:8, :] = row_sums(ed[0, :, cols], eo[0, :, cols])[0:4, :]
-    dec_recv[x] = dec_src[x]
-
     pl.semaphore_wait(barrier, len(partners))
 
     st_out = [remote(st_src.at[:, at_x(d)], st_all.at[mp, x], st_s.at[d], st_r.at[mp, x], dev(x_=at_x(d)))
               for d in (1, 3, 2)]
-    vg_out = [remote(vg_all.at[x], vg_all.at[x], vg_s.at[d], vg_r.at[x], dev(x_=at_x(d))) for d in (1, 3, 2)]
+
+    def vg_to(e, s, d):
+        return remote(vg_all.at[e, s], vg_all.at[e, s], vg_s.at[e, d], vg_r.at[e, s], dev(x_=at_x(d)))
+
     dec_out = [remote(dec_src.at[at_x(d)], dec_recv.at[x], dec_s.at[d], dec_r.at[x], dev(x_=at_x(d)))
                for d in (1, 3, 2)]
     for cp in st_out:
@@ -135,46 +131,102 @@
     mine, other = mp, oyl * 2 + c
     st_to_ylo(x).start()
     st_to_sibling(mine, 0, x).start()
-    for cp in vg_out:
-        cp.start()
-
-    enc_out = []
+
+    enc_out, st_out_args = [], []
     for i in range(2):
         e = (x + i) % 2
         xt = 2 * c + e
         cols = pl.ds(pl.multiple_of(e * HD, HD), HD)
         for a, src in ((0, ek), (1, ev)):
             enc_out.append((src.at[0, :, cols], kv.at[a, x], kv_s.at[i, a], kv_r.at[a, x],
-                            dev(x_=xt, c_=a), jnp.logical_and(xt == x, c == a)))
+                            dev(x_=xt, c_=a), jnp.logical_and(xt == x, c == a), 0))
         here = jnp.logical_and(xt == x, c == yh)
         target = dev(x_=xt, c_=yh)
         for a, src in ((0, eq), (1, ed)):
-            enc_out.append((src.at[0, :, cols], qd.at[x, a], qd_s.at[i, a], qd_r.at[x, a], target, here))
-        enc_out.append((stats_src.at[e], stats.at[x], sta_s.at[i], sta_r.at[x], target, here))
-    for args in enc_out:
-        push(*args)
-    for cp in dec_out:
-        cp.start()
-
-    for d in (1, 3, 2):
-        s = at_x(d)
-        arrived(st_all.at[mine, s], st_r.at[mine, s])
-        st_to_ylo(s).start()
-        st_to_sibling(mine, 0, s).start()
-    for d in ORDER:
-        s = at_x(d)
-        arrived(st_all.at[other, s], st_r.at[other, s])
-        st_to_sibling(other, 1, s).start()
-
-    for d in (1, 3, 2):
-        s = at_x(d)
-        arrived(dec_recv.at[s], dec_r.at[s])
-    total = dec_recv[0].astype(F32)
-    for s in range(1, NX):
-        total = total + dec_recv[s].astype(F32)
-    dec_mine[...] = total
-    dec_swap = remote(dec_mine, dec_other, decy_s, decy_r, yhi)
-    dec_swap.start()
+            enc_out.append((src.at[0, :, cols], qd.at[x, a], qd_s.at[i, a], qd_r.at[x, a], target, here, 1))
+        st_out_args.append((stats_src.at[e], stats.at[x], sta_s.at[i], sta_r.at[x], target, here))
+
+    qd_out, kv_out = [args for args in enc_out if args[6]], [args for args in enc_out if not args[6]]
+    qd_out, kv_out = [args[:6] for args in qd_out], [args[:6] for args in kv_out]
+
+    def send(some):
+        for args in some:
+            push(*args)
+
+    cross = []
+
+    def cross_values(e):
+        cols = slice(e * HD, (e + 1) * HD)
+        probs = jnp.exp(mm(ck_v[0, :, cols], dq_v[0, :, cols], 1, 1)) * (1.0 / dt_v[0, e:e + 1, :])
+        value_grad = mm(probs.astype(BF16), dd_v[0, :, cols], 1, 0).astype(BF16)
+        out_cv[0, :, cols] = value_grad
+        vg_all[e, x] = value_grad
+        cross.append(probs)
+
+    def send_values(e):
+        for d in (1, 3):
+            vg_to(e, x, d).start()
+        if not RELAY:
+            vg_to(e, x, 2).start()
+
+    def send_stats():
+        for cp in loads[7:]:
+            cp.wait()
+        for e in range(2):
+            cols = slice(e * HD, (e + 1) * HD)
+            stats_src[e, 0:4, :] = jnp.broadcast_to(1.0 / et_v[0, e:e + 1, :], (4, 256))
+            stats_src[e, 4:8, :] = row_sums(ed_v[0, :, cols], eo_v[0, :, cols])[0:4, :]
+        send(st_out_args)
+
+    def cross_rest():
+        for e in range(2):
+            cols = slice(e * HD, (e + 1) * HD)
+            keys, query, grad = ck_v[0, :, cols], dq_v[0, :, cols], dd_v[0, :, cols]
+            delta = row_sums(grad, do_v[0, :, cols])[0:1, :]
+            dscores = (cross[e] * (mm(cv_v[0, :, cols], grad, 1, 1) - delta)).astype(BF16)
+            out_ck[0, :, cols] = mm(dscores, query, 1, 0).astype(BF16)
+            dec_src[:, :, cols] = mm(dscores, keys, 0, 0).astype(BF16).reshape(NX, 64, HD)
+        dec_recv[x] = dec_src[x]
+        for cp in dec_out:
+            cp.start()
+
+    def states_first():
+        for d in (1, 3, 2):
+            s = at_x(d)
+            arrived(st_all.at[mine, s], st_r.at[mine, s])
+            st_to_ylo(s).start()
+            st_to_sibling(mine, 0, s).start()
+
+    def states_second():
+        for d in ORDER:
+            s = at_x(d)
+            arrived(st_all.at[other, s], st_r.at[other, s])
+            st_to_sibling(other, 1, s).start()
+
+    def states_third():
+        for s in range(NX):
+            arrived(st_all.at[yl * 2 + oc, s], st_r.at[yl * 2 + oc, s])
+            arrived(st_all.at[oyl * 2 + oc, s], st_r.at[oyl * 2 + oc, s])
+
+    def relay(e):
+        return 1 + 2 * ((c + e) % 2)
+
+    def vg_relayed(e):
+        d = relay(e)
+        return remote(vg_all.at[e, (x + NX - d) % NX], vg_all.at[e, (x + NX - d) % NX], vg_s.at[e, 2],
+                      vg_r.at[e, (x + NX - d) % NX], dev(x_=at_x(d)))
+
+    def values_arrive(e):
+        if RELAY:
+            d = relay(e)
+            first = (x + NX - d) % NX
+            arrived(vg_all.at[e, first], vg_r.at[e, first])
+            vg_relayed(e).start()
+            arrived(vg_all.at[e, (x + d) % NX], vg_r.at[e, (x + d) % NX])
+            arrived(vg_all.at[e, at_x(2)], vg_r.at[e, at_x(2)])
+        else:
+            for d in (1, 3, 2):
+                arrived(vg_all.at[e, at_x(d)], vg_r.at[e, at_x(d)])
 
     def kv_to_sibling(s):
         return remote(kv.at[c, s], kv.at[c, s], kvc_s.at[s], kv_r.at[c, s], sibling)
@@ -189,36 +241,108 @@
         arrived(stats.at[s], sta_r.at[s])
 
     first_hand = c == yh
-    for d in ORDER:
-        s = at_x(d)
-        arrived(kv.at[c, s], kv_r.at[c, s])
-        kv_to_sibling(s).start()
-
-        @pl.when(first_hand)
-        def _(s=s):
-            qd_arrived(s)
-            for cp in qd_to_yhi(s):
-                cp.start()
-
-    for d in (1, 3, 2):
-        s = at_x(d)
-        arrived(vg_all.at[s], vg_r.at[s])
-    for s in range(NX):
-        arrived(st_all.at[yl * 2 + oc, s], st_r.at[yl * 2 + oc, s])
-        arrived(st_all.at[oyl * 2 + oc, s], st_r.at[oyl * 2 + oc, s])
-
+
+    dec_swap = remote(dec_mine, dec_other, decy_s, decy_r, yhi)
     z_out = []
-    for k in range(4):
-        m = (z // 2 + k) % 4
-        part = mm(st_all[m, 0].reshape(256, 256), vg_all[0], 1, 0)
+
+    def decoder_sum():
+        for d in (1, 3, 2):
+            s = at_x(d)
+            arrived(dec_recv.at[s], dec_r.at[s])
+        total = dec_recv[0].astype(F32)
         for s in range(1, NX):
-            part = part + mm(st_all[m, s].reshape(256, 256), vg_all[s], 1, 0)
-        z_src[k] = part.astype(BF16).reshape(2, 128, 512)
-        for l in range(2):
-            zt = 2 * m + l
-            args = (z_src.at[k, l], z_recv.at[z], z_s.at[k, l], z_r.at[z], dev(z_=zt), zt == z)
-            push(*args)
-            z_out.append(args)
+            total = total + dec_recv[s].astype(F32)
+        dec_mine[...] = total
+        dec_swap.start()
+
+    def queries_forward():
+        for d in ORDER:
+            s = at_x(d)
+
+            @pl.when(first_hand)
+            def _(s=s):
+                qd_arrived(s)
+                for cp in qd_to_yhi(s):
+                    cp.start()
+
+    def keys_forward():
+        for d in ORDER:
+            s = at_x(d)
+            arrived(kv.at[c, s], kv_r.at[c, s])
+            kv_to_sibling(s).start()
+
+    def weight_gradient(e):
+        for k in range(4):
+            m = (z // 2 + k) % 4
+            part = mm(st_all[m, 0].reshape(256, 256), vg_all[e, 0], 1, 0)
+            for s in range(1, NX):
+                part = part + mm(st_all[m, s].reshape(256, 256), vg_all[e, s], 1, 0)
+            z_src[e, k] = part.astype(BF16).reshape(2, 128, HD)
+            for l in range(2):
+                zt = 2 * m + l
+                args = (z_src.at[e, k, l], z_recv.at[e, z], z_s.at[e, k, l], z_r.at[e, z], dev(z_=zt), zt == z)
+                push(*args)
+                z_out.append(args)
+
+    for cp in loads[1:7]:
+        cp.wait()
+    if PLAN == 0:
+        cross_values(0)
+        send_values(0)
+        send(qd_out)
+        cross_values(1)
+        send_values(1)
+        send(kv_out)
+        send_stats()
+        cross_rest()
+        states_first()
+        states_second()
+        values_arrive(0)
+        states_third()
+        weight_gradient(0)
+        queries_forward()
+        values_arrive(1)
+        weight_gradient(1)
+        keys_forward()
+        decoder_sum()
+    elif PLAN == 1:
+        cross_values(0)
+        send_values(0)
+        cross_values(1)
+        send_stats()
+        states_first()
+        send(qd_out)
+        states_second()
+        values_arrive(0)
+        send_values(1)
+        states_third()
+        weight_gradient(0)
+        queries_forward()
+        send(kv_out)
+        values_arrive(1)
+        weight_gradient(1)
+        cross_rest()
+        keys_forward()
+        decoder_sum()
+    elif PLAN == 2:
+        send(qd_out)
+        cross_values(0)
+        send_values(0)
+        cross_values(1)
+        send_values(1)
+        send(kv_out)
+        send_stats()
+        cross_rest()
+        states_first()
+        queries_forward()
+        states_second()
+        values_arrive(0)
+        states_third()
+        weight_gradient(0)
+        values_arrive(1)
+        weight_gradient(1)
+        keys_forward()
+        decoder_sum()
 
     dec_swap.wait()
     dec_all[x] = (dec_mine[...] + dec_other[...]).astype(BF16)
@@ -295,14 +419,19 @@
             dq_fin[s] = (dq_own[s] + dq_recv[s].astype(F32)).astype(BF16)
             push(*dq_args(s))
 
-    for s in range(NZ):
-        arrived(z_recv.at[s], z_r.at[s])
-    w = z_recv[0].astype(F32)
-    for s in range(1, NZ):
-        w = w + z_recv[s].astype(F32)
-    y_src[...] = w.reshape(2, 64, 512)
-    y_swap = remote(y_src.at[oyh], y_recv, y_s, y_r, yhi)
-    y_swap.start()
+    def y_swap(e):
+        return remote(y_src.at[e, oyh], y_recv.at[e], y_s.at[e], y_r.at[e], yhi)
+
+    for e in range(2):
+        for s in range(NZ):
+            arrived(z_recv.at[e, s], z_r.at[e, s])
+        w = z_recv[e, 0].astype(F32)
+        for s in range(1, NZ):
+            w = w + z_recv[e, s].astype(F32)
+        w = w.reshape(2, 64, HD)
+        y_own[e] = w
+        y_src[e] = w.astype(y_src.dtype)
+        y_swap(e).start()
 
     for d in (1, 3, 2):
         s = at_x(d)
@@ -310,15 +439,14 @@
     out_dq[0] = dec_all[...].reshape(256, 512)
 
     for e in range(2):
-        cols = slice(e * HD, (e + 1) * HD)
-        for a, out in ((0, out_k), (1, out_v), (2, out_q)):
+        for a in range(3):
             arrived(raw.at[a, e], raw_r.at[a, e])
-            out[0, :, cols] = raw[a, e]
-
-    y_swap.wait()
-    out_w[...] = y_src[yh] + y_recv[...]
-
-    for cp in st_out + vg_out + dec_out + deca_out:
+
+    for e in range(2):
+        y_swap(e).wait()
+        out_w[:, e * HD:(e + 1) * HD] = y_own[e, yh] + y_recv[e].astype(F32)
+
+    for cp in st_out + dec_out + deca_out + ([vg_relayed(e) for e in range(2)] if RELAY else []):
         cp.wait_send()
     for d in range(NX):
         st_to_ylo(d).wait_send()
@@ -326,7 +454,10 @@
         st_to_sibling(other, 1, d).wait_send()
         kv_to_sibling(d).wait_send()
         acc_to_sibling(d).wait_send()
-    for args in enc_out + z_out + fin_out:
+    for e in range(2):
+        for d in (1, 3) if RELAY else (1, 3, 2):
+            vg_to(e, x, d).wait_send()
+    for args in qd_out + kv_out + st_out_args + z_out + fin_out:
         pushed(*args)
 
     @pl.when(first_hand)
@@ -342,39 +473,67 @@
             dq_to_yhi(s).wait_send()
 
 
+def finish(raw, in_ck, in_cv, in_dq, in_w, out_q, out_k, out_v, out_ck, out_cv, out_dq, out_w, sems):
+    copies = []
+    for a, out in ((0, out_k), (1, out_v), (2, out_q)):
+        for e in range(2):
+            copies.append((raw.at[a, e], out.at[0, :, e * HD:(e + 1) * HD]))
+    copies += [(in_ck, out_ck), (in_cv, out_cv), (in_dq, out_dq), (in_w, out_w)]
+    copies = [pltpu.make_async_copy(src, dst, sems.at[i]) for i, (src, dst) in enumerate(copies)]
+    for cp in copies:
+        cp.start()
+    for cp in copies:
+        cp.wait()
+
+
 def body(*arrays):
+    hbm = pl.BlockSpec(memory_space=pltpu.HBM)
     vmem = pl.BlockSpec(memory_space=pltpu.VMEM)
     dma = pltpu.SemaphoreType.DMA
-    outs = [jax.ShapeDtypeStruct((1, 256, 512), BF16) for _ in range(6)]
-    outs.append(jax.ShapeDtypeStruct((64, 512), F32))
+    grads = [((1, 256, 512), BF16)] * 3 + [((64, 512), F32)]
+    outs = [pltpu.VMEM((3, 2, 256, HD), BF16)] + [pltpu.VMEM(shape, dtype) for shape, dtype in grads]
+    buffers = [((1, 256, 1024), BF16)] + [((1, 256, 512), BF16)] * 5 + [((1, 2, 256), F32)]
+    buffers += [((1, 256, 512), BF16)] * 2 + [((1, 2, 256), F32)]
+    scratch = [pltpu.VMEM(shape, dtype) for shape, dtype in buffers] + [dma((10,))]
     buffers = [
-        ((4, NX, 64, 256), BF16), ((4, NX, 4, 64, 256), BF16), ((NX, 256, 512), BF16),
-        ((4, 2, 128, 512), BF16), ((NZ, 128, 512), BF16), ((2, 64, 512), F32), ((64, 512), F32),
+        ((4, NX, 64, 256), BF16), ((4, NX, 4, 64, 256), BF16), ((2, NX, 256, HD), BF16),
+        ((2, 4, 2, 128, HD), BF16), ((2, NZ, 128, HD), BF16), ((2, 2, 64, HD), F32), ((2, 2, 64, HD), SWAP),
+        ((2, 64, HD), SWAP),
         ((2, NX, 256, HD), BF16), ((NX, 2, 256, HD), BF16), ((2, 8, 256), F32), ((NX, 8, 256), F32),
         ((2, NX, 256, HD), F32), ((NX, 256, HD), F32), ((NX, 256, HD), BF16), ((NX, 256, HD), F32),
-        ((NX, 256, HD), BF16), ((NX, 256, HD), BF16), ((NX, 256, HD), BF16), ((3, 2, 256, HD), BF16),
+        ((NX, 256, HD), BF16), ((NX, 256, HD), BF16), ((NX, 256, HD), BF16),
         ((NX, 64, 512), BF16), ((NX, 64, 512), BF16), ((64, 512), F32), ((64, 512), F32), ((NX, 64, 512), BF16),
     ]
     semaphores = [
-        (NX,), (4, NX), (NX,), (2, NX), (NX,), (NX,), (4, 2), (NZ,), None, None,
+        (NX,), (4, NX), (NX,), (2, NX), (2, NX), (2, NX), (2, 4, 2), (2, NZ), (2,), (2,),
         (2, 2), (2, NX), (NX,), (2, 2), (NX, 2), (NX, 2), (2,), (NX,), (NX,),
         (NX,), (NX,), (NX,), (3, 2), (NX,), (NX,), (NX,),
         (NX,), (NX,), None, None, (NX,), (NX,),
     ]
-    scratch = [pltpu.VMEM(shape, dtype) for shape, dtype in buffers]
+    scratch += [pltpu.VMEM(shape, dtype) for shape, dtype in buffers]
     scratch += [dma if shape is None else dma(shape) for shape in semaphores]
-    return tuple(pl.pallas_call(
+    parts = pl.pallas_call(
         kernel,
         out_shape=outs,
-        in_specs=[vmem] * 13,
-        out_specs=[vmem] * 7,
+        in_specs=[hbm] * 13,
+        out_specs=[vmem] * 5,
         scratch_shapes=scratch,
         compiler_params=pltpu.CompilerParams(
-            collective_id=0, has_side_effects=True, vmem_limit_bytes=48 * 1024 * 1024
+            collective_id=0, has_side_effects=True, vmem_limit_bytes=40 * 1024 * 1024
         ),
         cost_estimate=pl.CostEstimate(flops=5_000_000_000, bytes_accessed=6_000_000, transcendentals=1_200_000),
         name="grads",
-    )(*arrays))
+    )(*[pltpu.with_memory_space_constraint(array, pltpu.HBM) for array in arrays])
+    shapes = [jax.ShapeDtypeStruct(shape, dtype) for shape, dtype in [((1, 256, 512), BF16)] * 3 + grads]
+    return tuple(pl.pallas_call(
+        finish,
+        out_shape=shapes,
+        in_specs=[vmem] * 5,
+        out_specs=[hbm] * 7,
+        scratch_shapes=[dma((10,))],
+        compiler_params=pltpu.CompilerParams(vmem_limit_bytes=2 * 1024 * 1024),
+        name="finish",
+    )(*[pltpu.with_memory_space_constraint(part, pltpu.VMEM) for part in parts]))
 
 
 def solution(mesh):

time: 95.3 us -> 69.3 us (0.73)
  local copies, waits for them, and re-layouts: 16.8 us -> 0 us
  Pallas kernels: 77.4 us -> 68.6 us
    unnamed x33 -> x0, local copies, waits for them, and re-layouts: 16.8 us -> none
    pallas_call x1 -> x2, Pallas kernels: 77.4 us -> 68.6 us  [the longest x1 67.3 us: body(): pl.pallas_call(kernel, out_shape=outs, in_specs=[hbm] * 13, out_specs=[vm...]
where the time goes in v2:
time: 69.3 us; the launch traced here: 69.2 us
  Pallas kernels  68.6 us (99%)
    pallas_call x1, Pallas kernels, body(): pl.pallas_call(kernel, out_shape=outs, in_specs=[hbm] * 13, out_specs=[vm...  67.3 us

profile of v2, /device:TPU:1, one launch (start us, length us, event | category | flops | bytes accessed | tf_op | source)
XLA Modules:
  0.0 69.2 jit_solution(5919854970951964064)
XLA Ops:
  0.6 67.3 %grads.1 = (bf16[3,2,256,256]{3,2,1,0:T(8,128)(2,1)S(1)}, bf16[1,256,512]{2,1,0:T(8,128)(2,1)S(1)}, bf16[1,256,512]{2,1,0:T(8,128)(2,1)S(1)}, bf16[1,256,512]{2,1,0:T(8,128)(2,1)S(1)}, f32[64,512]{1,0:T(8,128)S(1)}) custom-call(bf16[1,256,512]{2,1,0:T(8,128)(2,1)} %eq.1, bf16[1,256,512]{2,1,0:T(8,128)(2,1)} %ek.1, bf16[1,256,512]{2,1,0:T(8,128)(2,1)} %ev.1, ...), custom_call_target="tpu_custom_call" | custom-call | flops 5000000000 | bytes 6000000 | tf_op jit(solution)/shard_map/grads/pallas_call | solution.py:515
  68.0 1.3 %finish.1 = (bf16[1,256,512]{2,1,0:T(8,128)(2,1)}, bf16[1,256,512]{2,1,0:T(8,128)(2,1)}, bf16[1,256,512]{2,1,0:T(8,128)(2,1)}, bf16[1,256,512]{2,1,0:T(8,128)(2,...) custom-call(bf16[3,2,256,256]{3,2,1,0:T(8,128)(2,1)S(1)} %get-tuple-element.12.raw, ...), custom_call_target="tpu_custom_call" | custom-call | tf_op jit(solution)/shard_map/finish/pallas_call | solution.py:528

commit v3 on v2

--- a/solution.py
+++ b/solution.py
@@ -12,10 +12,7 @@
 BF16 = jnp.bfloat16
 MESH = pl.DeviceIdType.MESH
 ORDER = (0, 1, 3, 2)
-RELAY = False
-GATE = 0
 SWAP = F32
-PLAN = 1
 
 
 def mm(a, b, ca, cb):
@@ -64,7 +61,7 @@
     kv, qd, stats_src, stats, acc, acc_recv, fin, dq_own, dq_send, dq_recv, dq_fin,
     dec_src, dec_recv, dec_mine, dec_other, dec_all,
     st_s, st_r, sty_s, stc_s, vg_s, vg_r, z_s, z_r, y_s, y_r,
-    kv_s, kv_r, kvc_s, qd_s, qd_r, qdy_s, sta_s, sta_r, stay_s,
+    kv_s, kv_r, kvc_s, qd_s, qd_r, qdy_s, qdc_s, sta_s, sta_r, stay_s,
     acc_s, acc_r, fin_s, raw_r, dqy_s, dqy_r, dqo_s,
     dec_s, dec_r, decy_s, decy_r, deca_s, deca_r,
 ):
@@ -109,8 +106,6 @@
         st_src[k] = piece.reshape(NX, 64, 256)
     st_all[mp, x] = st_src[:, x]
 
-    pl.semaphore_wait(barrier, len(partners))
-
     st_out = [remote(st_src.at[:, at_x(d)], st_all.at[mp, x], st_s.at[d], st_r.at[mp, x], dev(x_=at_x(d)))
               for d in (1, 3, 2)]
 
@@ -119,9 +114,6 @@
 
     dec_out = [remote(dec_src.at[at_x(d)], dec_recv.at[x], dec_s.at[d], dec_r.at[x], dev(x_=at_x(d)))
                for d in (1, 3, 2)]
-    for cp in st_out:
-        cp.start()
-
     def st_to_ylo(s):
         return remote(st_all.at[mp, s], st_all.at[mp, s], sty_s.at[s], st_r.at[mp, s], ylo)
 
@@ -129,13 +121,10 @@
         return remote(st_all.at[m, s], st_all.at[m, s], stc_s.at[k, s], st_r.at[m, s], sibling)
 
     mine, other = mp, oyl * 2 + c
-    st_to_ylo(x).start()
-    st_to_sibling(mine, 0, x).start()
-
     enc_out, st_out_args = [], []
     for i in range(2):
-        e = (x + i) % 2
-        xt = 2 * c + e
+        e = (x // 2 + i) % 2
+        xt = c + 2 * e
         cols = pl.ds(pl.multiple_of(e * HD, HD), HD)
         for a, src in ((0, ek), (1, ev)):
             enc_out.append((src.at[0, :, cols], kv.at[a, x], kv_s.at[i, a], kv_r.at[a, x],
@@ -143,7 +132,8 @@
         here = jnp.logical_and(xt == x, c == yh)
         target = dev(x_=xt, c_=yh)
         for a, src in ((0, eq), (1, ed)):
-            enc_out.append((src.at[0, :, cols], qd.at[x, a], qd_s.at[i, a], qd_r.at[x, a], target, here, 1))
+            enc_out.append((src.at[0, :, cols], qd.at[0, x], qd_s.at[i, a], qd_r.at[0, x],
+                            dev(x_=xt, c_=a), jnp.logical_and(xt == x, c == a), 1))
         st_out_args.append((stats_src.at[e], stats.at[x], sta_s.at[i], sta_r.at[x], target, here))
 
     qd_out, kv_out = [args for args in enc_out if args[6]], [args for args in enc_out if not args[6]]
@@ -156,6 +146,9 @@
     cross = []
 
     def cross_values(e):
+        if e == 0:
+            for cp in loads[1:7]:
+                cp.wait()
         cols = slice(e * HD, (e + 1) * HD)
         probs = jnp.exp(mm(ck_v[0, :, cols], dq_v[0, :, cols], 1, 1)) * (1.0 / dt_v[0, e:e + 1, :])
         value_grad = mm(probs.astype(BF16), dd_v[0, :, cols], 1, 0).astype(BF16)
@@ -164,19 +157,16 @@
         cross.append(probs)
 
     def send_values(e):
-        for d in (1, 3):
+        for d in (1, 3, 2):
             vg_to(e, x, d).start()
-        if not RELAY:
-            vg_to(e, x, 2).start()
-
-    def send_stats():
+
+    def compute_stats():
         for cp in loads[7:]:
             cp.wait()
         for e in range(2):
             cols = slice(e * HD, (e + 1) * HD)
             stats_src[e, 0:4, :] = jnp.broadcast_to(1.0 / et_v[0, e:e + 1, :], (4, 256))
             stats_src[e, 4:8, :] = row_sums(ed_v[0, :, cols], eo_v[0, :, cols])[0:4, :]
-        send(st_out_args)
 
     def cross_rest():
         for e in range(2):
@@ -187,15 +177,12 @@
             out_ck[0, :, cols] = mm(dscores, query, 1, 0).astype(BF16)
             dec_src[:, :, cols] = mm(dscores, keys, 0, 0).astype(BF16).reshape(NX, 64, HD)
         dec_recv[x] = dec_src[x]
-        for cp in dec_out:
-            cp.start()
-
-    def states_first():
-        for d in (1, 3, 2):
-            s = at_x(d)
-            arrived(st_all.at[mine, s], st_r.at[mine, s])
-            st_to_ylo(s).start()
-            st_to_sibling(mine, 0, s).start()
+
+    def states_step(d):
+        s = at_x(d)
+        arrived(st_all.at[mine, s], st_r.at[mine, s])
+        st_to_ylo(s).start()
+        st_to_sibling(mine, 0, s).start()
 
     def states_second():
         for d in ORDER:
@@ -208,37 +195,22 @@
             arrived(st_all.at[yl * 2 + oc, s], st_r.at[yl * 2 + oc, s])
             arrived(st_all.at[oyl * 2 + oc, s], st_r.at[oyl * 2 + oc, s])
 
-    def relay(e):
-        return 1 + 2 * ((c + e) % 2)
-
-    def vg_relayed(e):
-        d = relay(e)
-        return remote(vg_all.at[e, (x + NX - d) % NX], vg_all.at[e, (x + NX - d) % NX], vg_s.at[e, 2],
-                      vg_r.at[e, (x + NX - d) % NX], dev(x_=at_x(d)))
-
-    def values_arrive(e):
-        if RELAY:
-            d = relay(e)
-            first = (x + NX - d) % NX
-            arrived(vg_all.at[e, first], vg_r.at[e, first])
-            vg_relayed(e).start()
-            arrived(vg_all.at[e, (x + d) % NX], vg_r.at[e, (x + d) % NX])
-            arrived(vg_all.at[e, at_x(2)], vg_r.at[e, at_x(2)])
-        else:
-            for d in (1, 3, 2):
-                arrived(vg_all.at[e, at_x(d)], vg_r.at[e, at_x(d)])
+    def value_arrives(e, d):
+        arrived(vg_all.at[e, at_x(d)], vg_r.at[e, at_x(d)])
 
     def kv_to_sibling(s):
         return remote(kv.at[c, s], kv.at[c, s], kvc_s.at[s], kv_r.at[c, s], sibling)
 
+    half = (c + yh) % 2
+
     def qd_to_yhi(s):
-        return [remote(qd.at[s, a], qd.at[s, a], qdy_s.at[s, a], qd_r.at[s, a], yhi) for a in range(2)] + [
-            remote(stats.at[s], stats.at[s], stay_s.at[s], sta_r.at[s], yhi)]
-
-    def qd_arrived(s):
-        for a in range(2):
-            arrived(qd.at[s, a], qd_r.at[s, a])
-        arrived(stats.at[s], sta_r.at[s])
+        return remote(qd.at[0, s], qd.at[1, s], qdy_s.at[s], qd_r.at[1, s], yhi)
+
+    def qd_to_sibling(s):
+        return remote(qd.at[1 - half, s], qd.at[2, s], qdc_s.at[s], qd_r.at[2, s], sibling)
+
+    def stats_to_yhi(s):
+        return remote(stats.at[s], stats.at[s], stay_s.at[s], sta_r.at[s], yhi)
 
     first_hand = c == yh
 
@@ -255,100 +227,98 @@
         dec_mine[...] = total
         dec_swap.start()
 
+    def query_forward(d):
+        s = at_x(d)
+        arrived(qd.at[0, s], qd_r.at[0, s])
+        qd_to_yhi(s).start()
+
+        @pl.when(first_hand)
+        def _():
+            arrived(stats.at[s], sta_r.at[s])
+            stats_to_yhi(s).start()
+
+        @pl.when(jnp.logical_not(first_hand))
+        def _():
+            qd_to_sibling(s).start()
+
+    def query_second(d):
+        s = at_x(d)
+        arrived(qd.at[1, s], qd_r.at[1, s])
+
+        @pl.when(first_hand)
+        def _():
+            qd_to_sibling(s).start()
+
+    def key_forward(d):
+        s = at_x(d)
+        arrived(kv.at[c, s], kv_r.at[c, s])
+        kv_to_sibling(s).start()
+
     def queries_forward():
         for d in ORDER:
-            s = at_x(d)
-
-            @pl.when(first_hand)
-            def _(s=s):
-                qd_arrived(s)
-                for cp in qd_to_yhi(s):
-                    cp.start()
+            query_forward(d)
 
     def keys_forward():
         for d in ORDER:
-            s = at_x(d)
-            arrived(kv.at[c, s], kv_r.at[c, s])
-            kv_to_sibling(s).start()
+            key_forward(d)
 
     def weight_gradient(e):
-        for k in range(4):
-            m = (z // 2 + k) % 4
+        for m in range(4):
             part = mm(st_all[m, 0].reshape(256, 256), vg_all[e, 0], 1, 0)
             for s in range(1, NX):
                 part = part + mm(st_all[m, s].reshape(256, 256), vg_all[e, s], 1, 0)
-            z_src[e, k] = part.astype(BF16).reshape(2, 128, HD)
-            for l in range(2):
-                zt = 2 * m + l
-                args = (z_src.at[e, k, l], z_recv.at[e, z], z_s.at[e, k, l], z_r.at[e, z], dev(z_=zt), zt == z)
-                push(*args)
-                z_out.append(args)
-
-    for cp in loads[1:7]:
-        cp.wait()
-    if PLAN == 0:
-        cross_values(0)
-        send_values(0)
-        send(qd_out)
-        cross_values(1)
-        send_values(1)
-        send(kv_out)
-        send_stats()
-        cross_rest()
-        states_first()
-        states_second()
-        values_arrive(0)
-        states_third()
-        weight_gradient(0)
-        queries_forward()
-        values_arrive(1)
-        weight_gradient(1)
-        keys_forward()
-        decoder_sum()
-    elif PLAN == 1:
-        cross_values(0)
-        send_values(0)
-        cross_values(1)
-        send_stats()
-        states_first()
-        send(qd_out)
-        states_second()
-        values_arrive(0)
-        send_values(1)
-        states_third()
-        weight_gradient(0)
-        queries_forward()
-        send(kv_out)
-        values_arrive(1)
-        weight_gradient(1)
-        cross_rest()
-        keys_forward()
-        decoder_sum()
-    elif PLAN == 2:
-        send(qd_out)
-        cross_values(0)
-        send_values(0)
-        cross_values(1)
-        send_values(1)
-        send(kv_out)
-        send_stats()
-        cross_rest()
-        states_first()
-        queries_forward()
-        states_second()
-        values_arrive(0)
-        states_third()
-        weight_gradient(0)
-        values_arrive(1)
-        weight_gradient(1)
-        keys_forward()
-        decoder_sum()
-
-    dec_swap.wait()
-    dec_all[x] = (dec_mine[...] + dec_other[...]).astype(BF16)
-    deca_out = [remote(dec_all.at[x], dec_all.at[x], deca_s.at[d], deca_r.at[x], dev(x_=at_x(d))) for d in (1, 3, 2)]
-    for cp in deca_out:
-        cp.start()
+            z_src[e, 2 * m:2 * m + 2] = part.astype(BF16).reshape(2, 128, HD)
+        z_recv[e, z] = z_src[e, z]
+        for d in (4, 3, 5, 2, 6, 1, 7):
+            zt = (z + d) % NZ
+            cp = remote(z_src.at[e, zt], z_recv.at[e, z], z_s.at[e, d], z_r.at[e, z], dev(z_=zt))
+            cp.start()
+            z_out.append(cp)
+
+    pl.semaphore_wait(barrier, len(partners))
+
+    def own():
+        st_to_ylo(x).start()
+        st_to_sibling(mine, 0, x).start()
+
+    deca_out = []
+
+    def decoder_out():
+        dec_swap.wait()
+        dec_all[x] = (dec_mine[...] + dec_other[...]).astype(BF16)
+        for d in (1, 3, 2):
+            cp = remote(dec_all.at[x], dec_all.at[x], deca_s.at[d], deca_r.at[x], dev(x_=at_x(d)))
+            cp.start()
+            deca_out.append(cp)
+
+    def start(copies):
+        for cp in copies:
+            cp.start()
+
+    start(st_out[:2])
+    own()
+    start(st_out[2:])
+    cross_values(0)
+    compute_stats()
+    send(qd_out)
+    send(st_out_args)
+    states_step(1)
+    states_step(3)
+    states_step(2)
+    cross_values(1)
+    send_values(0)
+    send(kv_out)
+    cross_rest()
+    queries_forward()
+    states_second()
+    value_arrives(0, 1)
+    value_arrives(0, 3)
+    value_arrives(0, 2)
+    states_third()
+    weight_gradient(0)
+    keys_forward()
+    send_values(1)
+    start(dec_out)
 
     for s in range(NX):
         arrived(kv.at[oc, s], kv_r.at[oc, s])
@@ -362,11 +332,14 @@
     for i, d in enumerate(ORDER):
         s = at_x(d)
 
+        query_second(d)
+
         @pl.when(jnp.logical_not(first_hand))
         def _(s=s):
-            qd_arrived(s)
-
-        query, grad = qd[s, 0], qd[s, 1]
+            arrived(stats.at[s], sta_r.at[s])
+
+        arrived(qd.at[2, s], qd_r.at[2, s])
+        query, grad = qd[half * (1 - c) + 2 * c, s], qd[half * c + 2 * (1 - c), s]
         inv, delta = stats[s, 0:1, :], stats[s, 4:5, :]
         grad_q = jnp.zeros((256, HD), F32)
         for h in range(2):
@@ -396,34 +369,47 @@
             dq_send[s] = grad_q.astype(BF16)
             dq_to_yhi(s).start()
 
-    e_of = x % 2
-    owner_c = x // 2
+    e_of = x // 2
+    owner_c = x % 2
     fin_out = []
-    for b in range(NX):
-        arrived(acc_recv.at[b], acc_r.at[b])
-        fin[b] = (acc[c, b] + acc_recv[b]).astype(BF16)
-        args = (fin.at[b], raw.at[c, e_of], fin_s.at[b], raw_r.at[c, e_of], dev(x_=b, c_=owner_c),
-                jnp.logical_and(b == x, c == owner_c))
-        push(*args)
-        fin_out.append(args)
+
+    def keys_back():
+        for b in range(NX):
+            arrived(acc_recv.at[b], acc_r.at[b])
+            fin[b] = (acc[c, b] + acc_recv[b]).astype(BF16)
+            args = (fin.at[b], raw.at[c, e_of], fin_s.at[b], raw_r.at[c, e_of], dev(x_=b, c_=owner_c),
+                    jnp.logical_and(b == x, c == owner_c))
+            push(*args)
+            fin_out.append(args)
 
     def dq_args(s):
         return (dq_fin.at[s], raw.at[2, e_of], dqo_s.at[s], raw_r.at[2, e_of], dev(x_=s, c_=owner_c),
                 jnp.logical_and(s == x, c == owner_c))
 
-    @pl.when(first_hand)
-    def _():
-        for d in ORDER:
-            s = at_x(d)
-            arrived(dq_recv.at[s], dqy_r.at[s])
-            dq_fin[s] = (dq_own[s] + dq_recv[s].astype(F32)).astype(BF16)
-            push(*dq_args(s))
+    def queries_back():
+        @pl.when(first_hand)
+        def _():
+            for d in ORDER:
+                s = at_x(d)
+                arrived(dq_recv.at[s], dqy_r.at[s])
+                dq_fin[s] = (dq_own[s] + dq_recv[s].astype(F32)).astype(BF16)
+                push(*dq_args(s))
+
+    keys_back()
+    queries_back()
+    value_arrives(1, 1)
+    value_arrives(1, 3)
+    value_arrives(1, 2)
+    weight_gradient(1)
+    decoder_sum()
+    decoder_out()
 
     def y_swap(e):
         return remote(y_src.at[e, oyh], y_recv.at[e], y_s.at[e], y_r.at[e], yhi)
 
     for e in range(2):
-        for s in range(NZ):
+        for d in (1, 7, 2, 6, 3, 5, 4):
+            s = (z + d) % NZ
             arrived(z_recv.at[e, s], z_r.at[e, s])
         w = z_recv[e, 0].astype(F32)
         for s in range(1, NZ):
@@ -446,7 +432,7 @@
         y_swap(e).wait()
         out_w[:, e * HD:(e + 1) * HD] = y_own[e, yh] + y_recv[e].astype(F32)
 
-    for cp in st_out + dec_out + deca_out + ([vg_relayed(e) for e in range(2)] if RELAY else []):
+    for cp in st_out + dec_out + deca_out + z_out:
         cp.wait_send()
     for d in range(NX):
         st_to_ylo(d).wait_send()
@@ -455,16 +441,19 @@
         kv_to_sibling(d).wait_send()
         acc_to_sibling(d).wait_send()
     for e in range(2):
-        for d in (1, 3) if RELAY else (1, 3, 2):
+        for d in (1, 3, 2):
             vg_to(e, x, d).wait_send()
-    for args in qd_out + kv_out + st_out_args + z_out + fin_out:
+    for args in qd_out + kv_out + st_out_args + fin_out:
         pushed(*args)
+
+    for s in range(NX):
+        qd_to_yhi(s).wait_send()
+        qd_to_sibling(s).wait_send()
 
     @pl.when(first_hand)
     def _():
         for s in range(NX):
-            for cp in qd_to_yhi(s):
-                cp.wait_send()
+            stats_to_yhi(s).wait_send()
             pushed(*dq_args(s))
 
     @pl.when(jnp.logical_not(first_hand))
@@ -497,20 +486,20 @@
     scratch = [pltpu.VMEM(shape, dtype) for shape, dtype in buffers] + [dma((10,))]
     buffers = [
         ((4, NX, 64, 256), BF16), ((4, NX, 4, 64, 256), BF16), ((2, NX, 256, HD), BF16),
-        ((2, 4, 2, 128, HD), BF16), ((2, NZ, 128, HD), BF16), ((2, 2, 64, HD), F32), ((2, 2, 64, HD), SWAP),
+        ((2, NZ, 128, HD), BF16), ((2, NZ, 128, HD), BF16), ((2, 2, 64, HD), F32), ((2, 2, 64, HD), SWAP),
         ((2, 64, HD), SWAP),
-        ((2, NX, 256, HD), BF16), ((NX, 2, 256, HD), BF16), ((2, 8, 256), F32), ((NX, 8, 256), F32),
+        ((2, NX, 256, HD), BF16), ((3, NX, 256, HD), BF16), ((2, 8, 256), F32), ((NX, 8, 256), F32),
         ((2, NX, 256, HD), F32), ((NX, 256, HD), F32), ((NX, 256, HD), BF16), ((NX, 256, HD), F32),
         ((NX, 256, HD), BF16), ((NX, 256, HD), BF16), ((NX, 256, HD), BF16),
         ((NX, 64, 512), BF16), ((NX, 64, 512), BF16), ((64, 512), F32), ((64, 512), F32), ((NX, 64, 512), BF16),
     ]
     semaphores = [
-        (NX,), (4, NX), (NX,), (2, NX), (2, NX), (2, NX), (2, 4, 2), (2, NZ), (2,), (2,),
-        (2, 2), (2, NX), (NX,), (2, 2), (NX, 2), (NX, 2), (2,), (NX,), (NX,),
+        (NX,), (4, NX), (NX,), (2, NX), (2, NX), (2, NX), (2, NZ), (2, NZ), (2,), (2,),
+        (2, 2), (2, NX), (NX,), (2, 2), (3, NX), (NX,), (NX,), (2,), (NX,), (NX,),
         (NX,), (NX,), (NX,), (3, 2), (NX,), (NX,), (NX,),
         (NX,), (NX,), None, None, (NX,), (NX,),
     ]
-    scratch += [pltpu.VMEM(shape, dtype) for shape, dtype in buffers]
+    scratch += [pltpu.VMEM(*buffer) for buffer in buffers]
     scratch += [dma if shape is None else dma(shape) for shape in semaphores]
     parts = pl.pallas_call(
         kernel,

time: 69.3 us -> 64 us (0.924)
  Pallas kernels: 68.6 us -> 63.2 us
    pallas_call x1, Pallas kernels: 67.3 us -> 62 us  [body(): pl.pallas_call(kernel, out_shape=outs, in_specs=[hbm] * 13, out_specs=[vm...]
where the time goes in v3:
time: 64 us; the launch traced here: 63.9 us
  Pallas kernels  63.2 us (99%)
  between operations  0.65 us (1%)
    pallas_call x1, Pallas kernels, body(): pl.pallas_call(kernel, out_shape=outs, in_specs=[hbm] * 13, out_specs=[vm...  62 us

profile of v3, /device:TPU:1, one launch (start us, length us, event | category | flops | bytes accessed | tf_op | source)
XLA Modules:
  0.0 63.9 jit_solution(2700669908540765367)
XLA Ops:
  0.6 62.0 %grads.1 = (bf16[3,2,256,256]{3,2,1,0:T(8,128)(2,1)S(1)}, bf16[1,256,512]{2,1,0:T(8,128)(2,1)S(1)}, bf16[1,256,512]{2,1,0:T(8,128)(2,1)S(1)}, bf16[1,256,512]{2,1,0:T(8,128)(2,1)S(1)}, f32[64,512]{1,0:T(8,128)S(1)}) custom-call(bf16[1,256,512]{2,1,0:T(8,128)(2,1)} %eq.1, bf16[1,256,512]{2,1,0:T(8,128)(2,1)} %ek.1, bf16[1,256,512]{2,1,0:T(8,128)(2,1)} %ev.1, ...), custom_call_target="tpu_custom_call" | custom-call | flops 5000000000 | bytes 6000000 | tf_op jit(solution)/shard_map/grads/pallas_call | solution.py:504
  62.6 1.3 %finish.1 = (bf16[1,256,512]{2,1,0:T(8,128)(2,1)}, bf16[1,256,512]{2,1,0:T(8,128)(2,1)}, bf16[1,256,512]{2,1,0:T(8,128)(2,1)}, bf16[1,256,512]{2,1,0:T(8,128)(2,...) custom-call(bf16[3,2,256,256]{3,2,1,0:T(8,128)(2,1)S(1)} %get-tuple-element.12.raw, ...), custom_call_target="tpu_custom_call" | custom-call | tf_op jit(solution)/shard_map/finish/pallas_call | solution.py:517

commit v4 on v3

--- a/solution.py
+++ b/solution.py
@@ -12,7 +12,6 @@
 BF16 = jnp.bfloat16
 MESH = pl.DeviceIdType.MESH
 ORDER = (0, 1, 3, 2)
-SWAP = F32
 
 
 def mm(a, b, ca, cb):
@@ -63,7 +62,7 @@
     st_s, st_r, sty_s, stc_s, vg_s, vg_r, z_s, z_r, y_s, y_r,
     kv_s, kv_r, kvc_s, qd_s, qd_r, qdy_s, qdc_s, sta_s, sta_r, stay_s,
     acc_s, acc_r, fin_s, raw_r, dqy_s, dqy_r, dqo_s,
-    dec_s, dec_r, decy_s, decy_r, deca_s, deca_r,
+    dec_s, dec_r, decy_s, decy_r, deca_s, deca_r, near,
 ):
     z = lax.axis_index("dp")
     blk = lax.axis_index("blk")
@@ -90,7 +89,7 @@
     barrier = pltpu.get_barrier_semaphore()
     partners = [dev(x_=at_x(d), c_=(c + dc) % 2) for d in range(NX) for dc in range(2) if d or dc]
     partners += [yhi, ylo]
-    partners += [dev(z_=(z + d) % NZ) for d in range(1, NZ)]
+    partners += [dev(z_=(z + d) % NZ) for d in (1, NZ - 1)]
     for partner in partners:
         pl.semaphore_signal(barrier, inc=1, device_id=partner, device_id_type=MESH)
 
@@ -277,6 +276,14 @@
 
     pl.semaphore_wait(barrier, len(partners))
 
+    def greet():
+        for way, d in ((0, 1), (1, NZ - 1)):
+            pl.semaphore_signal(near.at[way], inc=1, device_id=dev(z_=(z + d) % NZ), device_id_type=MESH)
+
+    def greeted():
+        for way in range(2):
+            pl.semaphore_wait(near.at[way], 1)
+
     def own():
         st_to_ylo(x).start()
         st_to_sibling(mine, 0, x).start()
@@ -298,19 +305,25 @@
     start(st_out[:2])
     own()
     start(st_out[2:])
+    greet()
     cross_values(0)
     compute_stats()
     send(qd_out)
     send(st_out_args)
+    greeted()
+    greet()
     states_step(1)
     states_step(3)
     states_step(2)
     cross_values(1)
     send_values(0)
+    greeted()
+    greet()
     send(kv_out)
     cross_rest()
     queries_forward()
     states_second()
+    greeted()
     value_arrives(0, 1)
     value_arrives(0, 3)
     value_arrives(0, 2)
@@ -486,8 +499,8 @@
     scratch = [pltpu.VMEM(shape, dtype) for shape, dtype in buffers] + [dma((10,))]
     buffers = [
         ((4, NX, 64, 256), BF16), ((4, NX, 4, 64, 256), BF16), ((2, NX, 256, HD), BF16),
-        ((2, NZ, 128, HD), BF16), ((2, NZ, 128, HD), BF16), ((2, 2, 64, HD), F32), ((2, 2, 64, HD), SWAP),
-        ((2, 64, HD), SWAP),
+        ((2, NZ, 128, HD), BF16), ((2, NZ, 128, HD), BF16), ((2, 2, 64, HD), F32), ((2, 2, 64, HD), F32),
+        ((2, 64, HD), F32),
         ((2, NX, 256, HD), BF16), ((3, NX, 256, HD), BF16), ((2, 8, 256), F32), ((NX, 8, 256), F32),
         ((2, NX, 256, HD), F32), ((NX, 256, HD), F32), ((NX, 256, HD), BF16), ((NX, 256, HD), F32),
         ((NX, 256, HD), BF16), ((NX, 256, HD), BF16), ((NX, 256, HD), BF16),
@@ -501,6 +514,7 @@
     ]
     scratch += [pltpu.VMEM(*buffer) for buffer in buffers]
     scratch += [dma if shape is None else dma(shape) for shape in semaphores]
+    scratch += [pltpu.SemaphoreType.REGULAR((2,))]
     parts = pl.pallas_call(
         kernel,
         out_shape=outs,

time: 64 us -> 63.2 us (0.988)
  Pallas kernels: 63.2 us -> 62.4 us
    pallas_call x1, Pallas kernels: 62 us -> 61.1 us  [body(): pl.pallas_call(kernel, out_shape=outs, in_specs=[hbm] * 13, out_specs=[vm...]
where the time goes in v4:
time: 63.2 us; the launch traced here: 63.1 us
  Pallas kernels  62.4 us (99%)
  between operations  0.65 us (1%)
    pallas_call x1, Pallas kernels, body(): pl.pallas_call(kernel, out_shape=outs, in_specs=[hbm] * 13, out_specs=[vm...  61.1 us

profile of v4, /device:TPU:1, one launch (start us, length us, event | category | flops | bytes accessed | tf_op | source)
XLA Modules:
  0.0 63.1 jit_solution(6724903302080440498)
XLA Ops:
  0.6 61.1 %grads.1 = (bf16[3,2,256,256]{3,2,1,0:T(8,128)(2,1)S(1)}, bf16[1,256,512]{2,1,0:T(8,128)(2,1)S(1)}, bf16[1,256,512]{2,1,0:T(8,128)(2,1)S(1)}, bf16[1,256,512]{2,1,0:T(8,128)(2,1)S(1)}, f32[64,512]{1,0:T(8,128)S(1)}) custom-call(bf16[1,256,512]{2,1,0:T(8,128)(2,1)} %eq.1, bf16[1,256,512]{2,1,0:T(8,128)(2,1)} %ek.1, bf16[1,256,512]{2,1,0:T(8,128)(2,1)} %ev.1, ...), custom_call_target="tpu_custom_call" | custom-call | flops 5000000000 | bytes 6000000 | tf_op jit(solution)/shard_map/grads/pallas_call | solution.py:518
  61.8 1.3 %finish.1 = (bf16[1,256,512]{2,1,0:T(8,128)(2,1)}, bf16[1,256,512]{2,1,0:T(8,128)(2,1)}, bf16[1,256,512]{2,1,0:T(8,128)(2,1)}, bf16[1,256,512]{2,1,0:T(8,128)(2,...) custom-call(bf16[3,2,256,256]{3,2,1,0:T(8,128)(2,1)S(1)} %get-tuple-element.12.raw, ...), custom_call_target="tpu_custom_call" | custom-call | tf_op jit(solution)/shard_map/finish/pallas_call | solution.py:531
